TPU v7x, 32 devices: a whole 2x2x4 slice. The times are simulated.
32 devices in a mesh: dp: 8 (over y, x, core), mp: 4 (over z).
Axes of the slice: x: 2, y: 2, z: 4, core: 2. Of those that a mesh axis runs over, the one named last changes fastest.
Arguments:
- grad_square: bfloat16 [8, 3, 64, 8192], P('dp', None, None, 'mp'), may hold values from -6 to 6
- grad_narrow: bfloat16 [8, 2, 64, 1024], P('dp', None, None, 'mp'), may hold values from -6 to 6
- grad_wide: bfloat16 [8, 2, 64, 28672], P('dp', None, None, 'mp'), may hold values from -6 to 6
- error_square: float32 [8, 3, 64, 8192], P('dp', None, None, 'mp'), may hold values from -4 to 4
- error_narrow: float32 [8, 2, 64, 1024], P('dp', None, None, 'mp'), may hold values from -4 to 4
- error_wide: float32 [8, 2, 64, 28672], P('dp', None, None, 'mp'), may hold values from -4 to 4
- basis_square: float32 [3, 8192, 32], P(None, 'mp'), may hold values from -0.0625 to 0.0625
- basis_narrow: float32 [2, 1024, 32], P(None, 'mp'), may hold values from -0.1875 to 0.1875
- basis_wide: float32 [2, 28672, 32], P(None, 'mp'), may hold values from -0.03125 to 0.03125
Outputs:
- new_error_square: float32 [8, 3, 64, 8192], P('dp', None, None, 'mp')
- new_error_narrow: float32 [8, 2, 64, 1024], P('dp', None, None, 'mp')
- new_error_wide: float32 [8, 2, 64, 28672], P('dp', None, None, 'mp')
- new_basis_square: float32 [3, 8192, 32], P(None, 'mp')
- new_basis_narrow: float32 [2, 1024, 32], P(None, 'mp')
- new_basis_wide: float32 [2, 28672, 32], P(None, 'mp')
- left_basis: float32 [7, 64, 32], replicated
All inputs are finite; a program needn't handle non-finite values.
Results may differ from a plain program's by a relative error of at most 0.0003.
Values sent between devices are 32-bit elements; how exact they have to be, the bound alone decides.
No kernel may reach another device: no remote copies, remote signals or barrier semaphores. Data moves between devices by JAX's collectives and lax.ppermute only.
A program may use at most 64 MiB of HBM per device.

v0:
```python
import jax
import jax.numpy as jnp
from jax import lax
from jax.sharding import PartitionSpec as P


def solve_rows(factor, product):

    def solve_one(lower_factor, rows):
        return jax.scipy.linalg.solve_triangular(lower_factor, rows.T, lower=True).T

    return jax.vmap(solve_one)(factor, product)


def gram_of(product):
    return jnp.einsum("mrk,mrl->mkl", product, product, precision=lax.Precision.HIGHEST)


def right_partial(merged, left_part):
    return jnp.einsum("mrc,mrk->mck", merged, left_part, precision=lax.Precision.HIGHEST)


def error_update(merged, left_part, new_basis):
    approx = jnp.einsum("mrk,mck->mrc", left_part, new_basis, precision=lax.Precision.HIGHEST)
    return (merged - approx)[None]


def per_device(
    grad_square,
    grad_narrow,
    grad_wide,
    error_square,
    error_narrow,
    error_wide,
    basis_square,
    basis_narrow,
    basis_wide,
):
    merged_square = grad_square[0].astype(jnp.float32) + error_square[0]
    merged_narrow = grad_narrow[0].astype(jnp.float32) + error_narrow[0]
    merged_wide = grad_wide[0].astype(jnp.float32) + error_wide[0]
    partial_value = jnp.concatenate(
        [
            jnp.einsum(
                "mrc,mck->mrk", merged_square, basis_square, precision=lax.Precision.HIGHEST
            ),
            jnp.einsum(
                "mrc,mck->mrk", merged_narrow, basis_narrow, precision=lax.Precision.HIGHEST
            ),
            jnp.einsum("mrc,mck->mrk", merged_wide, basis_wide, precision=lax.Precision.HIGHEST),
        ],
        axis=0,
    )
    product = lax.psum(partial_value, ("dp", "mp"))
    left_basis = solve_rows(jnp.linalg.cholesky(gram_of(product)), product)
    left_square = left_basis[0:3]
    left_narrow = left_basis[3:5]
    left_wide = left_basis[5:7]
    next_square, next_narrow, next_wide = lax.psum(
        (
            right_partial(merged_square, left_square),
            right_partial(merged_narrow, left_narrow),
            right_partial(merged_wide, left_wide),
        ),
        "dp",
    )
    new_square = error_update(merged_square, left_square, next_square)
    new_narrow = error_update(merged_narrow, left_narrow, next_narrow)
    new_wide = error_update(merged_wide, left_wide, next_wide)
    return (new_square, new_narrow, new_wide, next_square, next_narrow, next_wide, left_basis)


def solution(mesh):
    in_specs = (
        P("dp", None, None, "mp"),
        P("dp", None, None, "mp"),
        P("dp", None, None, "mp"),
        P("dp", None, None, "mp"),
        P("dp", None, None, "mp"),
        P("dp", None, None, "mp"),
        P(None, "mp", None),
        P(None, "mp", None),
        P(None, "mp", None),
    )
    out_specs = (
        P("dp", None, None, "mp"),
        P("dp", None, None, "mp"),
        P("dp", None, None, "mp"),
        P(None, "mp", None),
        P(None, "mp", None),
        P(None, "mp", None),
        P(),
    )
    return jax.shard_map(
        per_device, mesh=mesh, in_specs=in_specs, out_specs=out_specs, check_vma=False
    )
```

profile of v0, /device:TPU:0, one launch (start us, length us, event | category | flops | bytes accessed | tf_op | source)
XLA Modules:
  0.0 206.7 jit_solution(4344660954755627493)
XLA Ops:
  7.2 0.0 copy-start
  7.2 0.0 all-reduce.3.cloned.1.call-start
  7.3 1.3 fusion.13
  8.6 0.2 copy-done
  8.8 5.2 %fusion.3 = f32[2,64,32]{1,2,0:T(8,128)S(1)} fusion(f32[2,7168,32]{1,2,0:T(8,128)S(1)} %copy-done, f32[1,2,64,7168]{3,2,1,0:T(8,128)} %param.14, bf16[1,2,64,7168]{3,2,1,0:T(8,128)(2,1)} %param.11), kind=kOutput, calls=%fused_computation.4 | convolution fusion | flops 354156544 | bytes 7356416 | tf_op jit(solution)/shard_map/mrc,mck->mrk/dot_general | solution.py:50
  14.0 0.0 copy-done.3
  14.0 1.5 fusion.8
  15.6 0.7 pad_maximum_fusion
  16.2 43.0 %psum.28 = f32[7,64,32]{1,2,0:T(8,128)S(1)} all-reduce(f32[7,64,32]{1,2,0:T(8,128)} %pad_maximum_fusion), channel_id=1, replica_groups=mesh['dp'=8,'mp'=4] {'dp','mp'}, use_global_device_ids=true, to_apply=%region_0.0 | all-reduce | flops 14336 | bytes 114688 | tf_op jit(solution)/shard_map/psum | solution.py:54
  59.2 0.0 copy-start.8
  59.2 1.0 fusion.21
  60.2 1.6 copy.18
  61.8 1.6 fusion.17
  63.4 21.8 %custom-call.8 = f32[7,32,32]{2,1,0:T(8,128)} custom-call(f32[7,32,32]{2,1,0:T(8,128)} %fusion.17), custom_call_target="Cholesky" | custom-call | tf_op jit(solution)/shard_map/jit(cholesky)/cholesky | solution.py:55
  85.3 0.9 select_reduce_fusion
  86.2 0.1 compare_reduce_fusion
  86.3 1.6 select_bitcast_fusion
  87.9 18.6 %custom-call.9 = f32[7,1,32,32]{2,3,1,0:T(8,128)} custom-call(f32[7,1,32,32]{3,2,1,0:T(8,128)} %select_bitcast_fusion), custom_call_target="InvertDiagBlocksLowerTriangular" | custom-call | tf_op jit(solution)/shard_map/vmap(jit(_solve_triangular))/triangular_solve | solution.py:10
  106.5 1.5 fusion.15
  108.0 0.0 copy-start.7
  108.0 1.8 fusion.11
  109.8 3.1 %fusion.6 = f32[3,2048,32]{1,2,0:T(8,128)} fusion(f32[1,3,64,2048]{3,2,1,0:T(8,128)S(1)} %copy-done.3, bf16[1,3,64,2048]{3,2,1,0:T(8,128)(2,1)} %param.9, f32[7,64,32]{1,2,0:T(8,128)S(1)} %fusion.15), kind=kOutput, calls=%fused_computation.9 | convolution fusion | flops 151781376 | bytes 3194880 | tf_op jit(solution)/shard_map/mrc,mrk->mck/dot_general | solution.py:20
  112.9 5.1 %fusion.1 = f32[2,7168,32]{1,2,0:T(8,128)} fusion(f32[1,2,64,7168]{3,2,1,0:T(8,128)S(1)} %copy-done.1, bf16[1,2,64,7168]{3,2,1,0:T(8,128)(2,1)} %param.11, f32[7,64,32]{1,2,0:T(8,128)S(1)} %fusion.15), kind=kOutput, calls=%fused_computation.2 | convolution fusion | flops 354156544 | bytes 7372800 | tf_op jit(solution)/shard_map/mrc,mrk->mck/dot_general | solution.py:20
  118.0 0.0 all-reduce.3.cloned.1.call-update
  118.0 65.6 %all-reduce.3.cloned.1.call-done = (f32[3,2048,32]{1,2,0:T(8,128)}, f32[2,256,32]{1,2,0:T(8,128)}, f32[2,7168,32]{1,2,0:T(8,128)}) async-done(((f32[3,2048,32]{1,2,0:T(8,128)}, f32[2,256,32]{1,2,0:T(8,128)}, f32[2,7168,32]{1,2,0:T(8,128)}), (f32[3,2048,32]{1,2,0:T(8,128)}, f32[2,256,32]{1,2,0:T(8,128)}, f32[2,7168,32]{1,2,0:T(8,128)})) %all-reduce.3.cloned.1.call-update) | async-done | bytes 2686992 | tf_op jit(solution)/shard_map/psum | solution.py:59
  183.6 1.9 fusion.10
  185.5 4.1 %fusion.5 = f32[1,3,64,2048]{3,2,1,0:T(8,128)} fusion(f32[7,64,32]{1,2,0:T(8,128)S(1)} %fusion.15, f32[3,2048,32]{1,2,0:T(8,128)} %get-tuple-element.13, f32[1,3,64,2048]{3,2,1,0:T(8,128)S(1)} %copy-done.3, bf16[1,3,64,2048]{3,2,1,0:T(8,128)(2,1)} %param.9), kind=kOutput, calls=%fused_computation.8 | convolution fusion | flops 152174592 | bytes 4775936 | tf_op jit(solution)/shard_map/mrk,mck->mrc/dot_general | solution.py:24
  189.7 7.5 %fusion = f32[1,2,64,7168]{3,2,1,0:T(8,128)} fusion(f32[7,64,32]{1,2,0:T(8,128)S(1)} %fusion.15, f32[2,7168,32]{1,2,0:T(8,128)} %get-tuple-element.15, f32[1,2,64,7168]{3,2,1,0:T(8,128)S(1)} %copy-done.2, bf16[1,2,64,7168]{3,2,1,0:T(8,128)(2,1)} %param.11), kind=kOutput, calls=%fused_computation.1 | convolution fusion | flops 355074048 | bytes 11067392 | tf_op jit(solution)/shard_map/mrk,mck->mrc/dot_general | solution.py:24
  197.1 0.0 copy-done.6
  197.1 0.9 copy.24
  198.0 0.6 copy.25
  198.7 1.2 copy.26
  (18 shorter events, 0.0 us)
Async XLA Ops:
  7.2 1.6 copy-start
  7.2 176.4 %all-reduce.3.cloned.1.call-start = ((), (), s32[]{:S(2)}) async-start(), calls=%async_computation | async-start | bytes 5373952 | tf_op jit(solution)/shard_map/psum | solution.py:59
  8.8 5.2 %copy-start.3 = (f32[1,3,64,2048]{3,2,1,0:T(8,128)S(1)}, f32[1,3,64,2048]{3,2,1,0:T(8,128)}, u32[]{:S(2)}) copy-start(f32[1,3,64,2048]{3,2,1,0:T(8,128)} %param.12) | copy-start | bytes 4718596
  8.8 5.2 %copy-start.5 = (bf16[1,3,64,2048]{3,2,1,0:T(8,128)(2,1)S(1)}, bf16[1,3,64,2048]{3,2,1,0:T(8,128)(2,1)}, u32[]{:S(2)}) copy-start(bf16[1,3,64,2048]{3,2,1,0:T(8,128)(2,1)} %param.9) | copy-start | bytes 2359300
  8.8 5.2 %copy-start.9 = (f32[3,2048,32]{1,2,0:T(8,128)S(1)}, f32[3,2048,32]{1,2,0:T(8,128)}, u32[]{:S(2)}) copy-start(f32[3,2048,32]{1,2,0:T(8,128)} %param.15) | copy-start | bytes 2359300
  59.2 28.7 %copy-start.8 = (f32[7,64,32]{1,2,0:T(8,128)}, f32[7,64,32]{1,2,0:T(8,128)S(1)}, u32[]{:S(2)}) copy-start(f32[7,64,32]{1,2,0:T(8,128)S(1)} %psum.28) | copy-start | bytes 172036
  106.5 6.4 %copy-start.1 = (f32[1,2,64,7168]{3,2,1,0:T(8,128)S(1)}, f32[1,2,64,7168]{3,2,1,0:T(8,128)}, u32[]{:S(2)}) copy-start(f32[1,2,64,7168]{3,2,1,0:T(8,128)} %param.14) | copy-start | bytes 11010052
  108.0 81.7 %copy-start.7 = (f32[7,64,32]{1,2,0:T(8,128)}, f32[7,64,32]{1,2,0:T(8,128)S(1)}, u32[]{:S(2)}) copy-start(f32[7,64,32]{1,2,0:T(8,128)S(1)} %fusion.15) | copy-start | bytes 172036
  185.5 4.1 %copy-start.2 = (f32[1,2,64,7168]{3,2,1,0:T(8,128)S(1)}, f32[1,2,64,7168]{3,2,1,0:T(8,128)}, u32[]{:S(2)}) copy-start(f32[1,2,64,7168]{3,2,1,0:T(8,128)} %param.14) | copy-start | bytes 11010052
  189.7 7.5 %copy-start.6 = (f32[3,2048,32]{1,2,0:T(8,128)S(1)}, f32[3,2048,32]{1,2,0:T(8,128)}, u32[]{:S(2)}) copy-start(f32[3,2048,32]{1,2,0:T(8,128)} %get-tuple-element.13) | copy-start | bytes 2359300
  189.7 8.4 %copy-start.10 = (f32[2,256,32]{1,2,0:T(8,128)S(1)}, f32[2,256,32]{1,2,0:T(8,128)}, u32[]{:S(2)}) copy-start(f32[2,256,32]{1,2,0:T(8,128)} %get-tuple-element.14) | copy-start | bytes 196612
  189.7 9.0 %copy-start.4 = (f32[2,7168,32]{1,2,0:T(8,128)S(1)}, f32[2,7168,32]{1,2,0:T(8,128)}, u32[]{:S(2)}) copy-start(f32[2,7168,32]{1,2,0:T(8,128)} %get-tuple-element.15) | copy-start | bytes 5505028
Sparse Core Ops, SparseCore 0:
  118.1 65.4 all-reduce.2
where the time goes:
time: 207 us
  waiting for transfers between devices  65.6 us (32%)
  other arithmetic  45.4 us (22%)
  blocking collectives  43 us (21%)
  matrix products  33.9 us (16%)
  between operations  14.2 us (7%)
  local copies, waits for them, and re-layouts  4.66 us (2%)
    psum x1, waiting for transfers between devices, per_device(): lax.psum((right_partial(merged_square, left_square), right_partial(merged...  65.6 us
    psum x1, blocking collectives, per_device(): product = lax.psum(partial_value, ('dp', 'mp'))  43 us
    another operation x4, other arithmetic, per_device(): left_basis = solve_rows(jnp.linalg.cholesky(gram_of(product)), product)  22.9 us
    another operation x3, other arithmetic, solve_one(): return jax.scipy.linalg.solve_triangular(lower_factor, rows.T, lower=True).T  20.2 us
    dot_general x3, matrix products, error_update(): jnp.einsum('mrk,mck->mrc', left_part, new_basis, precision=lax.Precision....  13.5 us
    dot_general x3, matrix products, right_partial(): jnp.einsum('mrc,mrk->mck', merged, left_part, precision=lax.Precision.HIG...  9.98 us
    dot_general x1, matrix products, per_device(): jnp.einsum('mrc,mck->mrk', merged_wide, basis_wide, precision=lax.Precisi...  5.19 us
  transfers between devices with their start and end apart: 1, of which 1 were waited for; matrix products, arithmetic and copies ran while one was open for 0% of the time, Pallas kernels for 0%

commit v1 on v0

v1 whole, which is shorter than its diff:
```python
import functools
import math

import jax
import jax.numpy as jnp
from jax import lax
from jax.experimental import pallas as pl
from jax.experimental.pallas import tpu as pltpu
from jax.sharding import PartitionSpec as P

LANES = 128
MIB = 1024 * 1024
F32 = jnp.float32
BF16 = jnp.bfloat16


def round_up(value, step):
    return -(-value // step) * step


def chunk_of(columns, most=1024):
    if columns % LANES:
        return columns
    width = min(columns, most) // LANES * LANES
    while columns % width:
        width -= LANES
    return width


def split2(value):
    high = value.astype(BF16)
    low = (value - high.astype(F32)).astype(BF16)
    return high, low


def dot_last(left, right):
    return lax.dot_general(left, right, (((1,), (1,)), ((), ())), preferred_element_type=F32)


def dot_plain(left, right):
    return lax.dot_general(left, right, (((1,), (0,)), ((), ())), preferred_element_type=F32)


def lane_slice(column, width):
    if isinstance(column, int):
        return pl.ds(column, width)
    return pl.ds(pl.multiple_of(column, LANES), width)


class Layout:
    def __init__(self, groups, dp_bits):
        self.groups = groups
        self.places = []
        self.starts = []
        self.firsts = []
        used = 0
        matrices = 0
        for count, columns in groups:
            self.firsts.append(matrices)
            self.places.append(used)
            for _ in range(count):
                self.starts.append(used)
                used += round_up(columns, LANES)
            matrices += count
        self.matrices = matrices
        self.used = used
        unit = 1 << max(1, dp_bits - 2)
        units = max(4, -(-used // (2 * unit * LANES)))
        self.half = units * unit * LANES
        self.packed = 2 * self.half
        self.cells = []
        offset = 0
        base = units // 8
        shares = [2 * base + 2, 2 * base + 2, 2 * base, units - 6 * base - 4]
        if base == 0 or shares[3] < 1:
            shares = [units // 4] * 3 + [units - 3 * (units // 4)]
        for cell, share in enumerate(shares):
            width = share * unit * LANES
            self.cells.append((offset, width, cell % 2))
            offset += width
        self.orders = (list(range(1, dp_bits)), list(range(dp_bits - 1, 0, -1)))
        self.columns = sum(count * columns for count, columns in groups)

    def granule(self, cell):
        offset, width, _ = self.cells[cell]
        return math.gcd(*self.starts, self.half, offset, width // 2)

    def segments(self, low, high, most):
        found = []
        for index, (count, columns) in enumerate(self.groups):
            for matrix in range(count):
                place = self.places[index] + matrix * round_up(columns, LANES)
                begin, end = max(low, place), min(high, place + columns)
                if begin < end:
                    width = chunk_of(end - begin, most)
                    found.append((index, matrix, begin - place, begin, width, (end - begin) // width))
        return found


def widen(value):
    rows, width = value.shape
    if width % LANES == 0:
        return value
    return jnp.concatenate([value, jnp.zeros((rows, round_up(width, LANES) - width), value.dtype)], axis=1)


def bit_of(bit):
    return (lax.axis_index("dp") >> bit) & 1


def params(limit=8):
    return pltpu.CompilerParams(vmem_limit_bytes=limit * MIB)


VMEM_SPEC = pl.BlockSpec(memory_space=pltpu.VMEM)
HBM_SPEC = pl.BlockSpec(memory_space=pltpu.HBM)


def in_hbm(values):
    return [pltpu.with_memory_space_constraint(value, pltpu.HBM) for value in values]


def odd_buffer(layout, rows):
    odd = [(count, columns) for count, columns in layout.groups if columns % LANES] or [(1, LANES)]
    return pltpu.VMEM((max(count for count, _ in odd), rows, max(columns for _, columns in odd)), F32)


def merge_and_project_kernel(layout, grad_refs, error_refs, basis_refs, merged_ref, send_ref, keep_ref, grad_bufs, basis_bufs, odd_ref, total, sems):
    rank = total.shape[1] // 2
    rows = total.shape[2] // 2
    plans = []
    slot = 0
    for segment in layout.segments(0, layout.used, 2048):
        plans.append((*segment, slot))
        slot += segment[-1]

    def copies_of(plan, at):
        index, matrix, column, place, width, _, base = plan
        where = (matrix, slice(None), lane_slice(column + at * width, width))
        error_to = odd_ref.at[matrix] if width % LANES else merged_ref.at[:, lane_slice(place + at * width, width)]
        return (
            pltpu.make_async_copy(grad_refs[index].at[(0,) + where], grad_bufs[index].at[where], sems.at[0, base + at]),
            pltpu.make_async_copy(error_refs[index].at[(0,) + where], error_to, sems.at[1, base + at]),
            pltpu.make_async_copy(basis_refs[index].at[where], basis_bufs[index].at[where], sems.at[2, base + at]),
        )

    for plan in plans:
        for at in range(plan[5]):
            for copy in copies_of(plan, at):
                copy.start()
    if layout.used < layout.packed:
        merged_ref[:, layout.used :] = jnp.zeros((rows, layout.packed - layout.used), F32)
    total[...] = jnp.zeros_like(total)
    for plan in plans:
        index, matrix, column, place, width, steps, _ = plan

        def body(at, carry, plan=plan, index=index, matrix=matrix, column=column, place=place, width=width):
            for copy in copies_of(plan, at):
                copy.wait()
            where = (matrix, slice(None), lane_slice(column + at * width, width))
            packed = (slice(None), lane_slice(place + at * width, round_up(width, LANES)))
            error = odd_ref[matrix] if width % LANES else merged_ref[packed]
            merged = error + grad_bufs[index][where].astype(F32)
            merged_ref[packed] = widen(merged)
            merged_parts = jnp.concatenate(split2(merged), axis=0)
            basis_parts = jnp.concatenate(split2(basis_bufs[index][where]), axis=0)
            total[layout.firsts[index] + matrix] += dot_last(basis_parts, merged_parts)
            return carry

        if steps == 1:
            body(0, 0)
        else:
            lax.fori_loop(0, steps, body, 0)
    core = bit_of(0)
    quarter = rank // 4
    for matrix in range(total.shape[0]):
        value = total[matrix]
        top = value[:rank, :rows] + value[:rank, rows:]
        top = top + (value[rank:, :rows] + value[rank:, rows:])
        quarters = [top[number * quarter : (number + 1) * quarter] for number in range(4)]
        halves = [jnp.concatenate(quarters[2 * half : 2 * half + 2], axis=1) for half in range(2)]
        send_ref[matrix] = jnp.where(core == 0, halves[1], halves[0])
        keep_ref[matrix] = jnp.where(core == 0, halves[0], halves[1])


def merge_and_project(layout, rank, rows, grads, errors, bases):
    def kernel(*refs):
        merge_and_project_kernel(layout, refs[0:3], refs[3:6], refs[6:9], *refs[9:12], refs[12:15], refs[15:18], *refs[18:])

    read = sum(value.size * value.dtype.itemsize for value in (*grads, *errors, *bases))
    slots = sum(segment[-1] for segment in layout.segments(0, layout.used, 2048))
    return pl.pallas_call(
        kernel,
        name="merge_and_project",
        out_shape=[pltpu.VMEM((rows, layout.packed), F32)]
        + [jax.ShapeDtypeStruct((layout.matrices, rank // 4, 2 * rows), F32)] * 2,
        in_specs=[HBM_SPEC] * 9,
        out_specs=[VMEM_SPEC] * 3,
        scratch_shapes=[pltpu.VMEM((count, rows, columns), BF16) for count, columns in layout.groups]
        + [pltpu.VMEM((count, rank, columns), F32) for count, columns in layout.groups]
        + [
            odd_buffer(layout, rows),
            pltpu.VMEM((layout.matrices, 2 * rank, 2 * rows), F32),
            pltpu.SemaphoreType.DMA((3, slots)),
        ],
        compiler_params=params(12),
        cost_estimate=pl.CostEstimate(flops=8 * rows * rank * layout.columns, bytes_accessed=read, transcendentals=0),
    )(*in_hbm(grads), *in_hbm(errors), *in_hbm(bases))


def take_half(layout, merged):
    def kernel(merged_ref, out_ref):
        out_ref[...] = merged_ref[:, lane_slice((1 - bit_of(0)) * layout.half, layout.half)]

    return add_call("take_half", kernel, [(merged.shape[0], layout.half)], [merged])[0]


def split_sum(layout, merged, received):
    rows = merged.shape[0]

    def kernel(merged_ref, received_ref, out_ref):
        own = bit_of(0) * layout.half
        total = merged_ref[:, lane_slice(own, layout.half)] + received_ref[...]
        out_ref[:rows], out_ref[rows:] = split2(total)

    return pl.pallas_call(
        kernel,
        name="split_sum",
        out_shape=jax.ShapeDtypeStruct((2 * rows, layout.half), BF16),
        in_specs=[VMEM_SPEC] * 2,
        out_specs=VMEM_SPEC,
        compiler_params=params(),
        cost_estimate=pl.CostEstimate(flops=rows * layout.half, bytes_accessed=1_000_000, transcendentals=0),
    )(merged, received)


def next_sum_kernel(layout, step, *refs):
    for part in range(2):
        kept_ref, received_ref = refs[2 * part : 2 * part + 2]
        width = kept_ref.shape[1] // 2
        which = bit_of(layout.orders[part][step])
        for out_ref, pick in zip(refs[4 + 2 * part : 6 + 2 * part], (1 - which, which)):
            where = (slice(None), lane_slice(pick * width, width))
            out_ref[...] = kept_ref[where] + received_ref[where]


def next_sum(layout, step, arrays):
    rows = arrays[0].shape[0]
    return pl.pallas_call(
        functools.partial(next_sum_kernel, layout, step),
        name="next_sum",
        out_shape=[jax.ShapeDtypeStruct((rows, arrays[2 * part].shape[1] // 2), F32) for part in range(2) for _ in range(2)],
        in_specs=[VMEM_SPEC] * 4,
        out_specs=[VMEM_SPEC] * 4,
        compiler_params=params(),
        cost_estimate=pl.CostEstimate(flops=rows * layout.half, bytes_accessed=1_000_000, transcendentals=0),
    )(*arrays)


def add_call(name, kernel, out_shapes, arrays):
    return pl.pallas_call(
        kernel,
        name=name,
        out_shape=[jax.ShapeDtypeStruct(shape, F32) for shape in out_shapes],
        in_specs=[VMEM_SPEC] * len(arrays),
        out_specs=[VMEM_SPEC] * len(out_shapes),
        compiler_params=params(),
        cost_estimate=pl.CostEstimate(
            flops=sum(rows * columns for rows, columns in out_shapes), bytes_accessed=1_000_000, transcendentals=0
        ),
    )(*arrays)


def last_sum(arrays):
    def kernel(*refs):
        for part in range(2):
            refs[4 + part][...] = refs[2 * part][...] + refs[2 * part + 1][...]

    return add_call("last_sum", kernel, [arrays[0].shape, arrays[2].shape], arrays)


def join(layout, step, pieces, received):
    shapes = [(piece.shape[0], 2 * piece.shape[1]) for piece in pieces]

    def kernel(*refs):
        for part in range(2):
            which = bit_of(layout.orders[part][step])
            width = refs[part].shape[1]
            refs[4 + part][:, lane_slice(which * width, width)] = refs[part][...]
            refs[4 + part][:, lane_slice((1 - which) * width, width)] = refs[2 + part][...]

    return add_call("join", kernel, shapes, (*pieces, *received))


def pack(blocks):
    def kernel(*refs):
        column = 0
        for ref in refs[:-1]:
            refs[-1][:, column : column + ref.shape[1]] = ref[...]
            column += ref.shape[1]

    shape = (blocks[0].shape[0], sum(block.shape[1] for block in blocks))
    return add_call("pack", kernel, [shape], blocks)[0]


def orthonormal_rows(product_t, block=4):
    matrices, rank, rows = product_t.shape
    gram = jnp.stack(
        [
            lax.dot_general(
                product_t[j], product_t[j], (((1,), (1,)), ((), ())), precision=lax.Precision.HIGHEST, preferred_element_type=F32
            )
            for j in range(matrices)
        ]
    )
    filler = jnp.zeros((matrices, rank, LANES - rank - rows), F32)
    work = jnp.concatenate([gram, filler, product_t], axis=2)
    done = []
    for first in range(0, rank, block):
        start = first % 8
        row_id = lax.broadcasted_iota(jnp.int32, (1, work.shape[1], 1), 1)
        columns = [jnp.broadcast_to(work[:, :, first + t : first + t + 1], work.shape) for t in range(block)]
        pivot_rows = [work[:, start + t : start + t + 1, :] for t in range(block)]
        scaled = []
        for t in range(block):
            at = start + t
            inverse = 1.0 / columns[t][:, at : at + 1, :]
            scaled.append(pivot_rows[t] * inverse)
            for s in range(t + 1, block):
                pivot_rows[s] = pivot_rows[s] - scaled[t] * columns[t][:, start + s : start + s + 1, :]
                columns[s] = columns[s] - columns[t] * (columns[s][:, at : at + 1, :] * inverse)
        change = columns[0] * scaled[0]
        for t in range(1, block):
            change = change + columns[t] * scaled[t]
        work = work - jnp.where(row_id >= start + block, change, 0.0)
        for t in range(block):
            work = jnp.where(row_id == start + t, pivot_rows[t], work)
        if start + block == 8:
            done.append(work[:, :8, :])
            work = work[:, 8:, :]
    work = jnp.concatenate(done, axis=1)
    row_id = lax.broadcasted_iota(jnp.int32, work.shape, 1)
    lane_id = lax.broadcasted_iota(jnp.int32, work.shape, 2)
    pivots = jnp.sum(jnp.where(row_id == lane_id, work, 0.0), axis=2, keepdims=True)
    return work[:, :, LANES - rows :] * (1.0 / jnp.sqrt(pivots))


def factor_kernel(layout, own_ref, other_ref, sums_ref, left_ref, *refs):
    outs, parts_ref = refs[:-1], refs[-1]
    rows = left_ref.shape[2]
    core = bit_of(0)
    own, other = (jnp.concatenate([ref[:, :, :rows], ref[:, :, rows:]], axis=1) for ref in (own_ref, other_ref))
    both = [jnp.where(core == 0, one, two) for one, two in ((own, other), (other, own))]
    left = orthonormal_rows(jnp.concatenate(both, axis=1))
    left_ref[...] = left
    high, low = split2(left)
    parts_ref[...] = jnp.concatenate([high, high, low], axis=2)
    for cell, (offset, width, part) in enumerate(layout.cells):
        which = bit_of(layout.orders[part][0])
        width //= 2
        for out_ref, pick in zip(outs[2 * cell : 2 * cell + 2], (1 - which, which)):
            begin = offset + pick * width
            for at in range(0, width, layout.granule(cell)):
                column = core * layout.half + begin + at
                matrix = sum((column >= start).astype(jnp.int32) for start in layout.starts[1:])
                value = sums_ref[:, lane_slice(begin + at, layout.granule(cell))]
                stacked = jnp.concatenate([value, value[:rows]], axis=0)
                out_ref[:, at : at + layout.granule(cell)] = dot_plain(parts_ref[matrix], stacked)


def factor(layout, rank, rows, own, other, sums):
    return pl.pallas_call(
        functools.partial(factor_kernel, layout),
        name="factor",
        out_shape=[jax.ShapeDtypeStruct((layout.matrices, rank, rows), F32)]
        + [jax.ShapeDtypeStruct((rank, width // 2), F32) for _, width, _ in layout.cells for _ in range(2)],
        in_specs=[VMEM_SPEC] * 3,
        out_specs=[VMEM_SPEC] * (1 + 2 * len(layout.cells)),
        scratch_shapes=[pltpu.VMEM((layout.matrices, rank, 3 * rows), BF16)],
        compiler_params=params(),
        cost_estimate=pl.CostEstimate(flops=8 * rows * rank * layout.half, bytes_accessed=10_000_000, transcendentals=0),
    )(own, other, sums)


def turn(left):
    matrices, rank, rows = left.shape

    def kernel(left_ref, out_ref):
        high, low = split2(left_ref[...])
        for j in range(matrices):
            parts = jnp.concatenate([high[j], high[j], low[j]], axis=0).astype(F32)
            out_ref[j] = parts.T.astype(BF16)

    return pl.pallas_call(
        kernel,
        name="turn",
        out_shape=pltpu.VMEM((matrices, rows, 3 * rank), BF16),
        in_specs=[VMEM_SPEC],
        out_specs=VMEM_SPEC,
        compiler_params=params(),
        cost_estimate=pl.CostEstimate(flops=100_000, bytes_accessed=100_000, transcendentals=0),
    )(left)


def update_kernel(layout, stage, turned_ref, merged_ref, right_refs, error_refs, basis_refs, right_buf, error_buf, odd_error, odd_basis, sems):
    core = bit_of(0)
    ends = []
    slot = 0
    for half_core in range(2):
        for offset, width, part in layout.cells:
            size = width // 2
            for number in range(2):
                low = half_core * layout.half + offset + number * size
                segments = layout.segments(low, low + size, 4096)
                shift = offset // 2 - low
                named = bit_of(layout.orders[part][0]) == number
                if stage == 2:
                    mine = core != half_core
                else:
                    mine = (core == half_core) & (named if stage == 0 else ~named)

                def copies_of(segment, base, at):
                    index, matrix, column, place, width, _ = segment
                    where = (matrix, slice(None), lane_slice(column + at * width, width))
                    packed = (slice(None), lane_slice(place + at * width, width))
                    odd = width % LANES
                    error_from = odd_error.at[matrix] if odd else error_buf.at[packed]
                    basis_from = odd_basis.at[matrix] if odd else right_buf.at[packed]
                    return (
                        pltpu.make_async_copy(error_from, error_refs[index].at[(0,) + where], sems.at[0, base + at]),
                        pltpu.make_async_copy(basis_from, basis_refs[index].at[where], sems.at[1, base + at]),
                    )

                def run(segments=segments, base=slot, named=named, shift=shift, copies_of=copies_of):
                    for segment in segments:
                        index, matrix, _, place, width, steps = segment
                        padded = round_up(width, LANES)

                        def body(at, carry, segment=segment, base=base, index=index, matrix=matrix, place=place, width=width, padded=padded):
                            source = (slice(None), lane_slice(place + shift + at * width, padded))
                            packed = (slice(None), lane_slice(place + at * width, padded))
                            right = right_refs[0][source]
                            if stage == 2:
                                right = jnp.where(named, right, right_refs[1][source])
                            right_buf[packed] = right
                            high, low = split2(right)
                            turned = turned_ref[layout.firsts[index] + matrix]
                            approx = dot_plain(turned, jnp.concatenate([high, low, high], axis=0))
                            error = merged_ref[packed] - approx
                            error_buf[packed] = error
                            if width < padded:
                                odd_error[matrix] = error[:, :width]
                                odd_basis[matrix] = right[:, :width]
                            for copy in copies_of(segment, base, at):
                                copy.start()
                            return carry

                        if steps == 1:
                            body(0, 0)
                        else:
                            lax.fori_loop(0, steps, body, 0)
                        base += steps

                def end(segments=segments, base=slot, copies_of=copies_of):
                    for segment in segments:
                        for at in range(segment[-1]):
                            for copy in copies_of(segment, base, at):
                                copy.wait()
                        base += segment[-1]

                pl.when(mine)(run)
                ends.append((mine, end))
                slot += sum(segment[-1] for segment in segments)
    for mine, end in ends:
        pl.when(mine)(end)


def update_error(layout, rank, stage, turned, merged, rights, before=()):
    rows = merged.shape[0]
    groups = len(layout.groups)
    ins = 2 + len(rights)

    def kernel(*refs):
        turned_ref, merged_ref, *right_refs = refs[:ins]
        refs = refs[ins + len(before) :]
        update_kernel(layout, stage, turned_ref, merged_ref, right_refs, refs[:groups], refs[groups : 2 * groups], *refs[2 * groups :])

    slots = 0
    for low in range(0, layout.packed, layout.half):
        for offset, width, _ in layout.cells:
            for begin in (low + offset, low + offset + width // 2):
                slots += sum(segment[-1] for segment in layout.segments(begin, begin + width // 2, 4096))
    return pl.pallas_call(
        kernel,
        name="update_" + ("first", "own", "other")[stage],
        out_shape=[jax.ShapeDtypeStruct((1, count, rows, columns), F32) for count, columns in layout.groups]
        + [jax.ShapeDtypeStruct((count, rank, columns), F32) for count, columns in layout.groups],
        in_specs=[VMEM_SPEC] * ins + [HBM_SPEC] * len(before),
        out_specs=[HBM_SPEC] * (2 * groups),
        input_output_aliases={ins + number: number for number in range(len(before))},
        scratch_shapes=[
            pltpu.VMEM((rank, layout.packed), F32),
            pltpu.VMEM((rows, layout.packed), F32),
            odd_buffer(layout, rows),
            odd_buffer(layout, rank),
            pltpu.SemaphoreType.DMA((2, slots)),
        ],
        compiler_params=params(12),
        cost_estimate=pl.CostEstimate(flops=100_000, bytes_accessed=40_000_000 if stage else 100_000, transcendentals=0),
    )(turned, merged, *rights, *before)


def swap(value, axis, size, bit):
    return lax.ppermute(value, axis, [(i, i ^ (1 << bit)) for i in range(size)])


def sum_over_bits(value, axis, size, bits):
    while bits:
        turns = [0]
        for bit in bits[:2]:
            turns = turns + [turn | (1 << bit) for turn in turns]
        bits = bits[2:]
        terms = [value] + [lax.ppermute(value, axis, [(i, i ^ turn) for i in range(size)]) for turn in turns[1:]]
        while len(terms) > 1:
            terms = [one + two for one, two in zip(terms[::2], terms[1::2])]
        value = terms[0]
    return value


def per_device(sizes, grad_square, grad_narrow, grad_wide, error_square, error_narrow, error_wide, basis_square, basis_narrow, basis_wide):
    dp, mp = sizes
    dp_bits = dp.bit_length() - 1
    mp_bits = mp.bit_length() - 1
    grads = (grad_square, grad_narrow, grad_wide)
    errors = (error_square, error_narrow, error_wide)
    bases = tuple(jnp.swapaxes(value, 1, 2) for value in (basis_square, basis_narrow, basis_wide))
    rows = grad_square.shape[2]
    rank = basis_square.shape[2]
    layout = Layout([(value.shape[1], value.shape[3]) for value in grads], dp_bits)
    order = lax.optimization_barrier
    steps = dp_bits - 1

    def swap_parts(values, step):
        return [swap(values[part], "dp", dp, layout.orders[part][step]) for part in range(2)]

    merged, send, product = merge_and_project(layout, rank, rows, grads, errors, bases)
    product = product + swap(send, "dp", dp, 0)
    merged, product = order((merged, product))
    received = swap(take_half(layout, merged), "dp", dp, 0)
    product = sum_over_bits(product, "dp", dp, list(range(1, dp_bits)))
    product = sum_over_bits(product, "mp", mp, list(range(mp_bits)))
    received, product = order((received, product))
    sums = split_sum(layout, merged, received)
    left, *arrays = factor(layout, rank, rows, product, swap(product, "dp", dp, 0), sums)
    turned = turn(left)

    chunks = [arrays[4 * chunk : 4 * chunk + 4] for chunk in range(2)]
    for step in range(max(1, steps - 1)):
        traded = [swap_parts(chunk[::2], step) for chunk in chunks]
        chunks = [[chunk[1], one, chunk[3], two] for chunk, (one, two) in zip(chunks, traded)]
        if step < steps - 2:
            chunks = [next_sum(layout, step + 1, chunk) for chunk in chunks]
    chunks = [last_sum(chunk) for chunk in chunks]
    if steps > 1:
        traded = [swap_parts(chunk, steps - 1) for chunk in chunks]
        first = last_sum([chunks[0][0], traded[0][0], chunks[0][1], traded[0][1]])
        one, two = order((*traded[1], *first))[:2]
        chunks = [first, last_sum([chunks[1][0], one, chunks[1][1], two])]
    for step in reversed(range(1, steps - 1)):
        chunks = [join(layout, step, chunk, swap_parts(chunk, step)) for chunk in chunks]
    news = [swap_parts(chunk, 0) for chunk in chunks]
    own = pack([piece for chunk in chunks for piece in chunk])
    first_other = swap(own, "dp", dp, 0)
    outs = update_error(layout, rank, 0, turned, merged, [own])
    tied = order((*outs, *news[0], *news[1]))
    outs, own = tied[: len(outs)], pack(tied[len(outs) :])
    other = swap(own, "dp", dp, 0)
    outs = update_error(layout, rank, 1, turned, merged, [own], outs)
    outs = update_error(layout, rank, 2, turned, merged, [first_other, other], outs)
    return (*outs[:3], *(jnp.swapaxes(value, 1, 2) for value in outs[3:]), jnp.swapaxes(left, 1, 2))


def solution(mesh):
    in_specs = (P("dp", None, None, "mp"),) * 6 + (P(None, "mp", None),) * 3
    out_specs = (P("dp", None, None, "mp"),) * 3 + (P(None, "mp", None),) * 3 + (P(),)
    sizes = (mesh.shape["dp"], mesh.shape["mp"])
    return jax.shard_map(
        functools.partial(per_device, sizes), mesh=mesh, in_specs=in_specs, out_specs=out_specs, check_vma=False
    )
```

time: 207 us -> 59.7 us (0.29)
  other arithmetic: 45.4 us -> 0.02 us
  waiting for transfers between devices: 65.6 us -> 20.3 us
  blocking collectives: 43 us -> 0 us
  matrix products: 33.9 us -> 0 us
  starting transfers between devices: 0.04 us -> 22.5 us
  Pallas kernels: 0 us -> 15.9 us
  between operations: 14.2 us -> 0.78 us
  local copies, waits for them, and re-layouts: 4.66 us -> 0.01 us
    psum x1 -> x0, waiting for transfers between devices: 65.6 us -> none  [per_device(): lax.psum((right_partial(merged_square, left_square), right_partial(merged...]
    another operation x7 -> x0, other arithmetic: 43.1 us -> none  [the longest x4 22.9 us: per_device(): left_basis = solve_rows(jnp.linalg.cholesky(gram_of(product)), product)]
    psum x1 -> x0, blocking collectives: 43 us -> none  [per_device(): product = lax.psum(partial_value, ('dp', 'mp'))]
    dot_general x10 -> x0, matrix products: 32.4 us -> none  [the longest x3 13.5 us: error_update(): jnp.einsum('mrk,mck->mrc', left_part, new_basis, precision=lax.Precision....]
    ppermute x0 -> x23, starting transfers between devices: none -> 22.5 us  [the longest x17 13.9 us: swap(): return lax.ppermute(value, axis, [(i, i ^ 1 << bit) for i in range(size)])]
    ppermute x0 -> x23, waiting for transfers between devices: none -> 20.3 us  [the longest x17 12.5 us: swap(): return lax.ppermute(value, axis, [(i, i ^ 1 << bit) for i in range(size)])]
    pallas_call x0 -> x14, Pallas kernels: none -> 15.9 us  [the longest x3 6.27 us: update_error(): pl.pallas_call(kernel, name='update_' + ('first', 'own', 'other')[stage],...]
    unnamed x25 -> x2, local copies, waits for them, and re-layouts: 3.02 us -> 0.01 us
  transfers between devices with their start and end apart: 1 -> 23, of which waited for: 1 -> 14; matrix products, arithmetic and copies ran while one was open for 0% -> 0% of each run, Pallas kernels for 0% -> 8%
where the time goes in v1:
time: 59.7 us; the launch traced here: 59.6 us
  starting transfers between devices  22.5 us (38%)
  waiting for transfers between devices  20.3 us (34%)
  Pallas kernels  15.9 us (27%)
  between operations  0.78 us (1%)
    ppermute x17, starting transfers between devices, swap(): return lax.ppermute(value, axis, [(i, i ^ 1 << bit) for i in range(size)])  13.9 us
    ppermute x17, waiting for transfers between devices, swap(): return lax.ppermute(value, axis, [(i, i ^ 1 << bit) for i in range(size)])  12.5 us
    ppermute x6, starting transfers between devices, sum_over_bits(): lax.ppermute(value, axis, [(i, i ^ turn) for i in range(size)])  8.62 us
    ppermute x6, waiting for transfers between devices, sum_over_bits(): lax.ppermute(value, axis, [(i, i ^ turn) for i in range(size)])  7.79 us
    pallas_call x3, Pallas kernels, update_error(): pl.pallas_call(kernel, name='update_' + ('first', 'own', 'other')[stage],...  6.27 us
    pallas_call x1, Pallas kernels, merge_and_project(): pl.pallas_call(kernel, name='merge_and_project', out_shape=[pltpu.VMEM((r...  5.46 us
    pallas_call x1, Pallas kernels, factor(): pl.pallas_call(functools.partial(factor_kernel, layout), name='factor', o...  3.05 us
  transfers between devices with their start and end apart: 23, of which 14 were waited for; matrix products, arithmetic and copies ran while one was open for 0% of the time, Pallas kernels for 8%

profile of v1, /device:TPU:0, one launch (start us, length us, event | category | flops | bytes accessed | tf_op | source)
XLA Modules:
  0.0 59.6 jit_solution(17687561444080619140)
XLA Ops:
  0.6 5.5 %merge_and_project.1 = (f32[64,20992]{1,0:T(8,128)S(1)}, f32[7,8,128]{2,1,0:T(8,128)S(1)}, f32[7,8,128]{2,1,0:T(8,128)S(1)}) custom-call(bf16[1,3,64,2048]{3,2,1,0:T(8,128)(2,1)} %refs_0_.1, bf16[1,2,64,256]{3,2,1,0:T(8,128)(2,1)} %refs_1_.1, bf16[1,2,64,7168]{3,2,1,0:T(8,128)(2,1)} %refs_2_.1, f32[1,3,64,2048]{3,2,1,0:T(8,128)} %refs_3_.1, ...), custom_call_target="tpu_custom_call" | custom-call | flops 343932928 | bytes 10747904 | tf_op jit(solution)/shard_map/merge_and_project/pallas_call | solution.py:192
  6.1 0.5 collective-permute-start
  6.6 0.9 %collective-permute-done = f32[7,8,128]{2,1,0:T(8,128)S(1)} collective-permute-done((f32[7,8,128]{2,1,0:T(8,128)S(1)}, f32[7,8,128]{2,1,0:T(8,128)S(1)}, u32[]{:S(2)}, u32[]{:S(2)}) %collective-permute-start) | collective-permute-done | bytes 28704 | tf_op jit(solution)/shard_map/ppermute | solution.py:514
  8.1 3.6 %collective-permute-start.4 = (f32[7,8,128]{2,1,0:T(8,128)S(1)}, f32[7,8,128]{2,1,0:T(8,128)S(1)}, u32[]{:S(2)}, u32[]{:S(2)}) collective-permute-start(f32[7,8,128]{2,1,0:T(8,128)S(1)} %add.21), channel_id=1, source_target_pairs={{0,24},{4,28},{8,16},{12,20},{16,8},{20,12},{24,0},{28,4},{1,25},{... | collective-permute-start | bytes 86024 | tf_op jit(solution)/shard_map/ppermute | solution.py:523
  12.2 1.3 %collective-permute-done.4 = f32[7,8,128]{2,1,0:T(8,128)S(1)} collective-permute-done((f32[7,8,128]{2,1,0:T(8,128)S(1)}, f32[7,8,128]{2,1,0:T(8,128)S(1)}, u32[]{:S(2)}, u32[]{:S(2)}) %collective-permute-start.4) | collective-permute-done | bytes 28704 | tf_op jit(solution)/shard_map/ppermute | solution.py:523
  13.5 2.0 %collective-permute-done.3 = f32[7,8,128]{2,1,0:T(8,128)S(1)} collective-permute-done((f32[7,8,128]{2,1,0:T(8,128)S(1)}, f32[7,8,128]{2,1,0:T(8,128)S(1)}, u32[]{:S(2)}, u32[]{:S(2)}) %collective-permute-start.3) | collective-permute-done | bytes 28704 | tf_op jit(solution)/shard_map/ppermute | solution.py:523
  16.1 3.7 %collective-permute-start.7 = (f32[7,8,128]{2,1,0:T(8,128)S(1)}, f32[7,8,128]{2,1,0:T(8,128)S(1)}, u32[]{:S(2)}, u32[]{:S(2)}) collective-permute-start(f32[7,8,128]{2,1,0:T(8,128)S(1)} %add_add_fusion.1), channel_id=1, source_target_pairs={{0,3},{1,2},{2,1},{3,0},{4,7},{5,6},{6,5},{7,4},{8,11},{9,10},{10,... | collective-permute-start | bytes 86024 | tf_op jit(solution)/shard_map/ppermute | solution.py:523
  19.7 0.8 %collective-permute-start.5 = (f32[7,8,128]{2,1,0:T(8,128)S(1)}, f32[7,8,128]{2,1,0:T(8,128)S(1)}, u32[]{:S(2)}, u32[]{:S(2)}) collective-permute-start(f32[7,8,128]{2,1,0:T(8,128)S(1)} %add_add_fusion.1), channel_id=1, source_target_pairs={{0,1},{1,0},{2,3},{3,2},{4,5},{5,4},{6,7},{7,6},{8,9},{9,8},{10,11... | collective-permute-start | bytes 86024 | tf_op jit(solution)/shard_map/ppermute | solution.py:523
  20.5 1.3 %collective-permute-done.7 = f32[7,8,128]{2,1,0:T(8,128)S(1)} collective-permute-done((f32[7,8,128]{2,1,0:T(8,128)S(1)}, f32[7,8,128]{2,1,0:T(8,128)S(1)}, u32[]{:S(2)}, u32[]{:S(2)}) %collective-permute-start.7) | collective-permute-done | bytes 28704 | tf_op jit(solution)/shard_map/ppermute | solution.py:523
  21.8 2.7 %collective-permute-done.6 = f32[7,8,128]{2,1,0:T(8,128)S(1)} collective-permute-done((f32[7,8,128]{2,1,0:T(8,128)S(1)}, f32[7,8,128]{2,1,0:T(8,128)S(1)}, u32[]{:S(2)}, u32[]{:S(2)}) %collective-permute-start.6) | collective-permute-done | bytes 28704 | tf_op jit(solution)/shard_map/ppermute | solution.py:523
  24.6 0.6 split_sum.1.sums_ref
  25.2 0.6 %collective-permute-done.8.other_ref = f32[7,8,128]{2,1,0:T(8,128)S(1)} collective-permute-done((f32[7,8,128]{2,1,0:T(8,128)S(1)}, f32[7,8,128]{2,1,0:T(8,128)S(1)}, u32[]{:S(2)}, u32[]{:S(2)}) %collective-permute-start.8) | collective-permute-done | bytes 28704 | tf_op jit(solution)/shard_map/ppermute | solution.py:514
  25.8 3.1 %factor.1 = (f32[7,32,64]{2,1,0:T(8,128)}, f32[32,1536]{1,0:T(8,128)S(1)}, f32[32,1536]{1,0:T(8,128)S(1)}, f32[32,1536]{1,0:T(8,128)S(1)}, f32[32,1536]{1,0:T(8,...) custom-call(f32[7,8,128]{2,1,0:T(8,128)S(1)} %add_add_fusion.own_ref,, ...), custom_call_target="tpu_custom_call" | custom-call | flops 171966464 | bytes 10000000 | tf_op jit(solution)/shard_map/factor/pallas_call | solution.py:372
  28.8 0.5 collective-permute-start.9
  29.4 1.5 %collective-permute-start.10 = (f32[32,1536]{1,0:T(8,128)S(1)}, f32[32,1536]{1,0:T(8,128)S(1)}, u32[]{:S(2)}, u32[]{:S(2)}) collective-permute-start(f32[32,1536]{1,0:T(8,128)S(1)} %get-tuple-element.72), channel_id=1, source_target_pairs={{0,16},{4,20},{8,24},{12,28},{16,0},{20,4},{24,8},{28,12},{1,17},{... | collective-permute-start | bytes 589832 | tf_op jit(solution)/shard_map/ppermute | solution.py:514
  30.9 1.5 %collective-permute-start.13 = (f32[32,1280]{1,0:T(8,128)S(1)}, f32[32,1280]{1,0:T(8,128)S(1)}, u32[]{:S(2)}, u32[]{:S(2)}) collective-permute-start(f32[32,1280]{1,0:T(8,128)S(1)} %get-tuple-element.78), channel_id=1, source_target_pairs={{0,8},{4,12},{8,0},{12,4},{16,24},{20,28},{24,16},{28,20},{1,9},{5... | collective-permute-start | bytes 491528 | tf_op jit(solution)/shard_map/ppermute | solution.py:514
  32.9 3.7 %collective-permute-done.9.refs_1_ = f32[32,1536]{1,0:T(8,128)S(1)} collective-permute-done((f32[32,1536]{1,0:T(8,128)S(1)}, f32[32,1536]{1,0:T(8,128)S(1)}, u32[]{:S(2)}, u32[]{:S(2)}) %collective-permute-start.9) | collective-permute-done | bytes 196640 | tf_op jit(solution)/shard_map/ppermute | solution.py:514
  36.6 0.6 collective-permute-done.10.refs_3_
  37.2 1.6 %collective-permute-start.11 = (f32[32,1536]{1,0:T(8,128)S(1)}, f32[32,1536]{1,0:T(8,128)S(1)}, u32[]{:S(2)}, u32[]{:S(2)}) collective-permute-start(f32[32,1536]{1,0:T(8,128)S(1)} %get-tuple-element.73.refs_0_), channel_id=1, source_target_pairs={{0,16},{4,20},{8,24},{12,28},{16,0},{20,4},{24,8},{28,12},{1,17},{... | collective-permute-start | bytes 589832 | tf_op jit(solution)/shard_map/ppermute | solution.py:514
  38.8 1.5 %collective-permute-start.12 = (f32[32,1536]{1,0:T(8,128)S(1)}, f32[32,1536]{1,0:T(8,128)S(1)}, u32[]{:S(2)}, u32[]{:S(2)}) collective-permute-start(f32[32,1536]{1,0:T(8,128)S(1)} %get-tuple-element.74.refs_2_), channel_id=1, source_target_pairs={{0,8},{4,12},{8,0},{12,4},{16,24},{20,28},{24,16},{28,20},{1,9},{5... | collective-permute-start | bytes 589832 | tf_op jit(solution)/shard_map/ppermute | solution.py:514
  40.4 1.4 %collective-permute-start.15 = (f32[32,1280]{1,0:T(8,128)S(1)}, f32[32,1280]{1,0:T(8,128)S(1)}, u32[]{:S(2)}, u32[]{:S(2)}) collective-permute-start(f32[32,1280]{1,0:T(8,128)S(1)} %get-tuple-element.81.refs_0_), channel_id=1, source_target_pairs={{0,16},{4,20},{8,24},{12,28},{16,0},{20,4},{24,8},{28,12},{1,17},{... | collective-permute-start | bytes 491528 | tf_op jit(solution)/shard_map/ppermute | solution.py:514
  41.7 0.6 %collective-permute-start.16 = (f32[32,896]{1,0:T(8,128)S(1)}, f32[32,896]{1,0:T(8,128)S(1)}, u32[]{:S(2)}, u32[]{:S(2)}) collective-permute-start(f32[32,896]{1,0:T(8,128)S(1)} %get-tuple-element.82.refs_2_), channel_id=1, source_target_pairs={{0,8},{4,12},{8,0},{12,4},{16,24},{20,28},{24,16},{28,20},{1,9},{5... | collective-permute-start | bytes 344072 | tf_op jit(solution)/shard_map/ppermute | solution.py:514
  42.3 2.3 %collective-permute-done.11.refs_1_ = f32[32,1536]{1,0:T(8,128)S(1)} collective-permute-done((f32[32,1536]{1,0:T(8,128)S(1)}, f32[32,1536]{1,0:T(8,128)S(1)}, u32[]{:S(2)}, u32[]{:S(2)}) %collective-permute-start.11) | collective-permute-done | bytes 196640 | tf_op jit(solution)/shard_map/ppermute | solution.py:514
  44.6 1.7 %collective-permute-done.12.refs_3_ = f32[32,1536]{1,0:T(8,128)S(1)} collective-permute-done((f32[32,1536]{1,0:T(8,128)S(1)}, f32[32,1536]{1,0:T(8,128)S(1)}, u32[]{:S(2)}, u32[]{:S(2)}) %collective-permute-start.12) | collective-permute-done | bytes 196640 | tf_op jit(solution)/shard_map/ppermute | solution.py:514
  46.4 1.2 %collective-permute-start.18 = (f32[32,1536]{1,0:T(8,128)S(1)}, f32[32,1536]{1,0:T(8,128)S(1)}, u32[]{:S(2)}, u32[]{:S(2)}) collective-permute-start(f32[32,1536]{1,0:T(8,128)S(1)} %get-tuple-element.75.refs_0_), channel_id=1, source_target_pairs={{0,8},{4,12},{8,0},{12,4},{16,24},{20,28},{24,16},{28,20},{1,9},{5... | collective-permute-start | bytes 589832 | tf_op jit(solution)/shard_map/ppermute | solution.py:514
  47.8 1.0 %collective-permute-done.16.refs_3_ = f32[32,896]{1,0:T(8,128)S(1)} collective-permute-done((f32[32,896]{1,0:T(8,128)S(1)}, f32[32,896]{1,0:T(8,128)S(1)}, u32[]{:S(2)}, u32[]{:S(2)}) %collective-permute-start.16) | collective-permute-done | bytes 114720 | tf_op jit(solution)/shard_map/ppermute | solution.py:514
  48.8 1.2 %collective-permute-start.20 = (f32[32,1280]{1,0:T(8,128)S(1)}, f32[32,1280]{1,0:T(8,128)S(1)}, u32[]{:S(2)}, u32[]{:S(2)}) collective-permute-start(f32[32,1280]{1,0:T(8,128)S(1)} %get-tuple-element.85.refs_2_), channel_id=1, source_target_pairs={{0,8},{4,12},{8,0},{12,4},{16,24},{20,28},{24,16},{28,20},{1,9},{5... | collective-permute-start | bytes 491528 | tf_op jit(solution)/shard_map/ppermute | solution.py:514
  50.0 1.0 %collective-permute-start.21 = (f32[32,896]{1,0:T(8,128)S(1)}, f32[32,896]{1,0:T(8,128)S(1)}, u32[]{:S(2)}, u32[]{:S(2)}) collective-permute-start(f32[32,896]{1,0:T(8,128)S(1)} %get-tuple-element.86.refs_3_), channel_id=1, source_target_pairs={{0,16},{4,20},{8,24},{12,28},{16,0},{20,4},{24,8},{28,12},{1,17},{... | collective-permute-start | bytes 344072 | tf_op jit(solution)/shard_map/ppermute | solution.py:514
  51.3 1.9 %update_first.1 = (f32[1,3,64,2048]{3,2,1,0:T(8,128)}, f32[1,2,64,256]{3,2,1,0:T(8,128)}, f32[1,2,64,7168]{3,2,1,0:T(8,128)}, f32[3,32,2048]{2,1,0:T(8,128)}, f3...) custom-call(bf16[7,64,96]{2,1,0:T(8,128)(2,1)S(1)} %turn.1.refs_0_, f32[64,20992]{1,0:T(8,128)S(1)} %get-tuple-element.64.merged_ref.refs_1_, ...), custom_call_target="tpu_custom_call" | custom-call | flops 100000 | bytes 100000 | tf_op jit(solution)/shard_map/update_first/pallas_call | solution.py:493
  53.2 1.6 %collective-permute-done.21.refs_3_ = f32[32,896]{1,0:T(8,128)S(1)} collective-permute-done((f32[32,896]{1,0:T(8,128)S(1)}, f32[32,896]{1,0:T(8,128)S(1)}, u32[]{:S(2)}, u32[]{:S(2)}) %collective-permute-start.21) | collective-permute-done | bytes 114720 | tf_op jit(solution)/shard_map/ppermute | solution.py:514
  54.9 1.9 %update_own.1 = (f32[1,3,64,2048]{3,2,1,0:T(8,128)}, f32[1,2,64,256]{3,2,1,0:T(8,128)}, f32[1,2,64,7168]{3,2,1,0:T(8,128)}, f32[3,32,2048]{2,1,0:T(8,128)}, f32[...) custom-call(bf16[7,64,96]{2,1,0:T(8,128)(2,1)S(1)} %turn.1.refs_0_, ...), custom_call_target="tpu_custom_call", output_to_operand_aliasing={{0}: (3, {}), {1}: (4, {}), {2}: (5, {}), {3}: (6, {}), {4}... | custom-call | flops 100000 | bytes 40000000 | tf_op jit(solution)/shard_map/update_own/pallas_call | solution.py:493
  57.0 2.5 %update_other.1 = (f32[1,3,64,2048]{3,2,1,0:T(8,128)}, f32[1,2,64,256]{3,2,1,0:T(8,128)}, f32[1,2,64,7168]{3,2,1,0:T(8,128)}, f32[3,32,2048]{2,1,0:T(8,128)}, f3...) custom-call(bf16[7,64,96]{2,1,0:T(8,128)(2,1)S(1)} %turn.1.refs_0_, ...), custom_call_target="tpu_custom_call", output_to_operand_aliasing={{0}: (4, {}), {1}: (5, {}), {2}: (6, {}), {3}: (7, {}), {4}... | custom-call | flops 100000 | bytes 40000000 | tf_op jit(solution)/shard_map/update_other/pallas_call | solution.py:493
  (33 shorter events, 3.3 us)
Async XLA Ops:
  6.1 1.4 %collective-permute-start = (f32[7,8,128]{2,1,0:T(8,128)S(1)}, f32[7,8,128]{2,1,0:T(8,128)S(1)}, u32[]{:S(2)}, u32[]{:S(2)}) collective-permute-start(f32[7,8,128]{2,1,0:T(8,128)S(1)} %get-tuple-element.63), channel_id=1, source_target_pairs={{0,4},{4,0},{8,12},{12,8},{16,20},{20,16},{24,28},{28,24},{1,5},{5... | collective-permute-start | bytes 86024 | tf_op jit(solution)/shard_map/ppermute | solution.py:514
  7.7 16.9 %collective-permute-start.1 = (f32[64,10496]{1,0:T(8,128)S(1)}, f32[64,10496]{1,0:T(8,128)S(1)}, u32[]{:S(2)}, u32[]{:S(2)}) collective-permute-start(f32[64,10496]{1,0:T(8,128)S(1)} %take_half.1), channel_id=1, source_target_pairs={{0,4},{4,0},{8,12},{12,8},{16,20},{20,16},{24,28},{28,24},{1,5},{5... | collective-permute-start | bytes 8060936 | tf_op jit(solution)/shard_map/ppermute | solution.py:514
  8.1 5.5 %collective-permute-start.4 = (f32[7,8,128]{2,1,0:T(8,128)S(1)}, f32[7,8,128]{2,1,0:T(8,128)S(1)}, u32[]{:S(2)}, u32[]{:S(2)}) collective-permute-start(f32[7,8,128]{2,1,0:T(8,128)S(1)} %add.21), channel_id=1, source_target_pairs={{0,24},{4,28},{8,16},{12,20},{16,8},{20,12},{24,0},{28,4},{1,25},{... | collective-permute-start | bytes 86024 | tf_op jit(solution)/shard_map/ppermute | solution.py:523
  11.7 3.9 %collective-permute-start.3 = (f32[7,8,128]{2,1,0:T(8,128)S(1)}, f32[7,8,128]{2,1,0:T(8,128)S(1)}, u32[]{:S(2)}, u32[]{:S(2)}) collective-permute-start(f32[7,8,128]{2,1,0:T(8,128)S(1)} %add.21), channel_id=1, source_target_pairs={{0,16},{4,20},{8,24},{12,28},{16,0},{20,4},{24,8},{28,12},{1,17},{... | collective-permute-start | bytes 86024 | tf_op jit(solution)/shard_map/ppermute | solution.py:523
  12.2 3.9 %collective-permute-start.2 = (f32[7,8,128]{2,1,0:T(8,128)S(1)}, f32[7,8,128]{2,1,0:T(8,128)S(1)}, u32[]{:S(2)}, u32[]{:S(2)}) collective-permute-start(f32[7,8,128]{2,1,0:T(8,128)S(1)} %add.21), channel_id=1, source_target_pairs={{0,8},{4,12},{8,0},{12,4},{16,24},{20,28},{24,16},{28,20},{1,9},{5... | collective-permute-start | bytes 86024 | tf_op jit(solution)/shard_map/ppermute | solution.py:523
  16.1 5.8 %collective-permute-start.7 = (f32[7,8,128]{2,1,0:T(8,128)S(1)}, f32[7,8,128]{2,1,0:T(8,128)S(1)}, u32[]{:S(2)}, u32[]{:S(2)}) collective-permute-start(f32[7,8,128]{2,1,0:T(8,128)S(1)} %add_add_fusion.1), channel_id=1, source_target_pairs={{0,3},{1,2},{2,1},{3,0},{4,7},{5,6},{6,5},{7,4},{8,11},{9,10},{10,... | collective-permute-start | bytes 86024 | tf_op jit(solution)/shard_map/ppermute | solution.py:523
  19.7 4.8 %collective-permute-start.6 = (f32[7,8,128]{2,1,0:T(8,128)S(1)}, f32[7,8,128]{2,1,0:T(8,128)S(1)}, u32[]{:S(2)}, u32[]{:S(2)}) collective-permute-start(f32[7,8,128]{2,1,0:T(8,128)S(1)} %add_add_fusion.1), channel_id=1, source_target_pairs={{0,2},{1,3},{2,0},{3,1},{4,6},{5,7},{6,4},{7,5},{8,10},{9,11},{10,... | collective-permute-start | bytes 86024 | tf_op jit(solution)/shard_map/ppermute | solution.py:523
  19.7 4.8 %collective-permute-start.5 = (f32[7,8,128]{2,1,0:T(8,128)S(1)}, f32[7,8,128]{2,1,0:T(8,128)S(1)}, u32[]{:S(2)}, u32[]{:S(2)}) collective-permute-start(f32[7,8,128]{2,1,0:T(8,128)S(1)} %add_add_fusion.1), channel_id=1, source_target_pairs={{0,1},{1,0},{2,3},{3,2},{4,5},{5,4},{6,7},{7,6},{8,9},{9,8},{10,11... | collective-permute-start | bytes 86024 | tf_op jit(solution)/shard_map/ppermute | solution.py:523
  24.5 1.3 %collective-permute-start.8 = (f32[7,8,128]{2,1,0:T(8,128)S(1)}, f32[7,8,128]{2,1,0:T(8,128)S(1)}, u32[]{:S(2)}, u32[]{:S(2)}) collective-permute-start(f32[7,8,128]{2,1,0:T(8,128)S(1)} %add_add_fusion.own_ref), channel_id=1, source_target_pairs={{0,4},{4,0},{8,12},{12,8},{16,20},{20,16},{24,28},{28,24},{1,5},{5... | collective-permute-start | bytes 86024 | tf_op jit(solution)/shard_map/ppermute | solution.py:514
  28.8 22.2 %copy-start = (f32[7,32,64]{2,1,0:T(8,128)S(1)}, f32[7,32,64]{2,1,0:T(8,128)}, u32[]{:S(2)}) copy-start(f32[7,32,64]{2,1,0:T(8,128)} %get-tuple-element.68.left_ref) | copy-start | bytes 172036
  28.8 7.7 %collective-permute-start.9 = (f32[32,1536]{1,0:T(8,128)S(1)}, f32[32,1536]{1,0:T(8,128)S(1)}, u32[]{:S(2)}, u32[]{:S(2)}) collective-permute-start(f32[32,1536]{1,0:T(8,128)S(1)} %get-tuple-element.70), channel_id=1, source_target_pairs={{0,8},{4,12},{8,0},{12,4},{16,24},{20,28},{24,16},{28,20},{1,9},{5... | collective-permute-start | bytes 589832 | tf_op jit(solution)/shard_map/ppermute | solution.py:514
  29.4 7.8 %collective-permute-start.10 = (f32[32,1536]{1,0:T(8,128)S(1)}, f32[32,1536]{1,0:T(8,128)S(1)}, u32[]{:S(2)}, u32[]{:S(2)}) collective-permute-start(f32[32,1536]{1,0:T(8,128)S(1)} %get-tuple-element.72), channel_id=1, source_target_pairs={{0,16},{4,20},{8,24},{12,28},{16,0},{20,4},{24,8},{28,12},{1,17},{... | collective-permute-start | bytes 589832 | tf_op jit(solution)/shard_map/ppermute | solution.py:514
  30.9 9.4 %collective-permute-start.13 = (f32[32,1280]{1,0:T(8,128)S(1)}, f32[32,1280]{1,0:T(8,128)S(1)}, u32[]{:S(2)}, u32[]{:S(2)}) collective-permute-start(f32[32,1280]{1,0:T(8,128)S(1)} %get-tuple-element.78), channel_id=1, source_target_pairs={{0,8},{4,12},{8,0},{12,4},{16,24},{20,28},{24,16},{28,20},{1,9},{5... | collective-permute-start | bytes 491528 | tf_op jit(solution)/shard_map/ppermute | solution.py:514
  32.4 7.9 %collective-permute-start.14 = (f32[32,896]{1,0:T(8,128)S(1)}, f32[32,896]{1,0:T(8,128)S(1)}, u32[]{:S(2)}, u32[]{:S(2)}) collective-permute-start(f32[32,896]{1,0:T(8,128)S(1)} %get-tuple-element.80), channel_id=1, source_target_pairs={{0,16},{4,20},{8,24},{12,28},{16,0},{20,4},{24,8},{28,12},{1,17},{... | collective-permute-start | bytes 344072 | tf_op jit(solution)/shard_map/ppermute | solution.py:514
  37.2 7.4 %collective-permute-start.11 = (f32[32,1536]{1,0:T(8,128)S(1)}, f32[32,1536]{1,0:T(8,128)S(1)}, u32[]{:S(2)}, u32[]{:S(2)}) collective-permute-start(f32[32,1536]{1,0:T(8,128)S(1)} %get-tuple-element.73.refs_0_), channel_id=1, source_target_pairs={{0,16},{4,20},{8,24},{12,28},{16,0},{20,4},{24,8},{28,12},{1,17},{... | collective-permute-start | bytes 589832 | tf_op jit(solution)/shard_map/ppermute | solution.py:514
  38.8 7.5 %collective-permute-start.12 = (f32[32,1536]{1,0:T(8,128)S(1)}, f32[32,1536]{1,0:T(8,128)S(1)}, u32[]{:S(2)}, u32[]{:S(2)}) collective-permute-start(f32[32,1536]{1,0:T(8,128)S(1)} %get-tuple-element.74.refs_2_), channel_id=1, source_target_pairs={{0,8},{4,12},{8,0},{12,4},{16,24},{20,28},{24,16},{28,20},{1,9},{5... | collective-permute-start | bytes 589832 | tf_op jit(solution)/shard_map/ppermute | solution.py:514
  40.4 8.4 %collective-permute-start.15 = (f32[32,1280]{1,0:T(8,128)S(1)}, f32[32,1280]{1,0:T(8,128)S(1)}, u32[]{:S(2)}, u32[]{:S(2)}) collective-permute-start(f32[32,1280]{1,0:T(8,128)S(1)} %get-tuple-element.81.refs_0_), channel_id=1, source_target_pairs={{0,16},{4,20},{8,24},{12,28},{16,0},{20,4},{24,8},{28,12},{1,17},{... | collective-permute-start | bytes 491528 | tf_op jit(solution)/shard_map/ppermute | solution.py:514
  41.7 7.1 %collective-permute-start.16 = (f32[32,896]{1,0:T(8,128)S(1)}, f32[32,896]{1,0:T(8,128)S(1)}, u32[]{:S(2)}, u32[]{:S(2)}) collective-permute-start(f32[32,896]{1,0:T(8,128)S(1)} %get-tuple-element.82.refs_2_), channel_id=1, source_target_pairs={{0,8},{4,12},{8,0},{12,4},{16,24},{20,28},{24,16},{28,20},{1,9},{5... | collective-permute-start | bytes 344072 | tf_op jit(solution)/shard_map/ppermute | solution.py:514
  46.4 8.4 %collective-permute-start.18 = (f32[32,1536]{1,0:T(8,128)S(1)}, f32[32,1536]{1,0:T(8,128)S(1)}, u32[]{:S(2)}, u32[]{:S(2)}) collective-permute-start(f32[32,1536]{1,0:T(8,128)S(1)} %get-tuple-element.75.refs_0_), channel_id=1, source_target_pairs={{0,8},{4,12},{8,0},{12,4},{16,24},{20,28},{24,16},{28,20},{1,9},{5... | collective-permute-start | bytes 589832 | tf_op jit(solution)/shard_map/ppermute | solution.py:514
  47.5 7.3 %collective-permute-start.19 = (f32[32,1536]{1,0:T(8,128)S(1)}, f32[32,1536]{1,0:T(8,128)S(1)}, u32[]{:S(2)}, u32[]{:S(2)}) collective-permute-start(f32[32,1536]{1,0:T(8,128)S(1)} %get-tuple-element.76.refs_1_), channel_id=1, source_target_pairs={{0,16},{4,20},{8,24},{12,28},{16,0},{20,4},{24,8},{28,12},{1,17},{... | collective-permute-start | bytes 589832 | tf_op jit(solution)/shard_map/ppermute | solution.py:514
  48.8 6.0 %collective-permute-start.20 = (f32[32,1280]{1,0:T(8,128)S(1)}, f32[32,1280]{1,0:T(8,128)S(1)}, u32[]{:S(2)}, u32[]{:S(2)}) collective-permute-start(f32[32,1280]{1,0:T(8,128)S(1)} %get-tuple-element.85.refs_2_), channel_id=1, source_target_pairs={{0,8},{4,12},{8,0},{12,4},{16,24},{20,28},{24,16},{28,20},{1,9},{5... | collective-permute-start | bytes 491528 | tf_op jit(solution)/shard_map/ppermute | solution.py:514
  50.0 4.8 %collective-permute-start.21 = (f32[32,896]{1,0:T(8,128)S(1)}, f32[32,896]{1,0:T(8,128)S(1)}, u32[]{:S(2)}, u32[]{:S(2)}) collective-permute-start(f32[32,896]{1,0:T(8,128)S(1)} %get-tuple-element.86.refs_3_), channel_id=1, source_target_pairs={{0,16},{4,20},{8,24},{12,28},{16,0},{20,4},{24,8},{28,12},{1,17},{... | collective-permute-start | bytes 344072 | tf_op jit(solution)/shard_map/ppermute | solution.py:514
  51.2 5.6 %collective-permute-start.17 = (f32[32,5248]{1,0:T(8,128)S(1)}, f32[32,5248]{1,0:T(8,128)S(1)}, u32[]{:S(2)}, u32[]{:S(2)}) collective-permute-start(f32[32,5248]{1,0:T(8,128)S(1)} %pack.2.refs_2_), channel_id=1, source_target_pairs={{0,4},{4,0},{8,12},{12,8},{16,20},{20,16},{24,28},{28,24},{1,5},{5... | collective-permute-start | bytes 2015240 | tf_op jit(solution)/shard_map/ppermute | solution.py:514
  54.9 2.2 %collective-permute-start.22 = (f32[32,5248]{1,0:T(8,128)S(1)}, f32[32,5248]{1,0:T(8,128)S(1)}, u32[]{:S(2)}, u32[]{:S(2)}) collective-permute-start(f32[32,5248]{1,0:T(8,128)S(1)} %pack.3.refs_2_), channel_id=1, source_target_pairs={{0,4},{4,0},{8,12},{12,8},{16,20},{20,16},{24,28},{28,24},{1,5},{5... | collective-permute-start | bytes 2015240 | tf_op jit(solution)/shard_map/ppermute | solution.py:514

commit v2 on v1

--- a/solution.py
+++ b/solution.py
@@ -402,77 +402,83 @@
     )(left)
 
 
+def update_regions(layout, stage):
+    regions = []
+    for half_core in range(2):
+        origin = half_core * layout.half
+        if stage == 2:
+            regions.append((half_core, None, [(origin, origin + layout.half, None)]))
+            continue
+        for bits in ((0, 0), (0, 1), (1, 0), (1, 1)):
+            ranges = []
+            for offset, width, part in layout.cells:
+                low = origin + offset + (bits[part] ^ stage) * (width // 2)
+                ranges.append((low, low + width // 2, offset // 2))
+            regions.append((half_core, bits, ranges))
+    return regions
+
+
+def update_chunks(layout, ranges):
+    for low, high, begin in ranges:
+        for index, matrix, column, place, width, steps in layout.segments(low, high, 2048):
+            for at in range(steps):
+                source = None if begin is None else begin + place - low + at * width
+                yield index, matrix, column + at * width, place + at * width, width, source
+
+
 def update_kernel(layout, stage, turned_ref, merged_ref, right_refs, error_refs, basis_refs, right_buf, error_buf, odd_error, odd_basis, sems):
     core = bit_of(0)
-    ends = []
-    slot = 0
-    for half_core in range(2):
-        for offset, width, part in layout.cells:
-            size = width // 2
-            for number in range(2):
-                low = half_core * layout.half + offset + number * size
-                segments = layout.segments(low, low + size, 4096)
-                shift = offset // 2 - low
-                named = bit_of(layout.orders[part][0]) == number
-                if stage == 2:
-                    mine = core != half_core
-                else:
-                    mine = (core == half_core) & (named if stage == 0 else ~named)
-
-                def copies_of(segment, base, at):
-                    index, matrix, column, place, width, _ = segment
-                    where = (matrix, slice(None), lane_slice(column + at * width, width))
-                    packed = (slice(None), lane_slice(place + at * width, width))
-                    odd = width % LANES
-                    error_from = odd_error.at[matrix] if odd else error_buf.at[packed]
-                    basis_from = odd_basis.at[matrix] if odd else right_buf.at[packed]
-                    return (
-                        pltpu.make_async_copy(error_from, error_refs[index].at[(0,) + where], sems.at[0, base + at]),
-                        pltpu.make_async_copy(basis_from, basis_refs[index].at[where], sems.at[1, base + at]),
-                    )
-
-                def run(segments=segments, base=slot, named=named, shift=shift, copies_of=copies_of):
-                    for segment in segments:
-                        index, matrix, _, place, width, steps = segment
-                        padded = round_up(width, LANES)
-
-                        def body(at, carry, segment=segment, base=base, index=index, matrix=matrix, place=place, width=width, padded=padded):
-                            source = (slice(None), lane_slice(place + shift + at * width, padded))
-                            packed = (slice(None), lane_slice(place + at * width, padded))
-                            right = right_refs[0][source]
-                            if stage == 2:
-                                right = jnp.where(named, right, right_refs[1][source])
-                            right_buf[packed] = right
-                            high, low = split2(right)
-                            turned = turned_ref[layout.firsts[index] + matrix]
-                            approx = dot_plain(turned, jnp.concatenate([high, low, high], axis=0))
-                            error = merged_ref[packed] - approx
-                            error_buf[packed] = error
-                            if width < padded:
-                                odd_error[matrix] = error[:, :width]
-                                odd_basis[matrix] = right[:, :width]
-                            for copy in copies_of(segment, base, at):
-                                copy.start()
-                            return carry
-
-                        if steps == 1:
-                            body(0, 0)
-                        else:
-                            lax.fori_loop(0, steps, body, 0)
-                        base += steps
-
-                def end(segments=segments, base=slot, copies_of=copies_of):
-                    for segment in segments:
-                        for at in range(segment[-1]):
-                            for copy in copies_of(segment, base, at):
-                                copy.wait()
-                        base += segment[-1]
-
-                pl.when(mine)(run)
-                ends.append((mine, end))
-                slot += sum(segment[-1] for segment in segments)
-    for mine, end in ends:
-        pl.when(mine)(end)
+    named = [bit_of(layout.orders[part][0]) for part in range(2)]
+
+    def copies_of(chunk, slot):
+        index, matrix, column, place, width, _ = chunk
+        where = (matrix, slice(None), pl.ds(column, width))
+        packed = (slice(None), pl.ds(place, width))
+        odd = width % LANES
+        error_from = odd_error.at[matrix] if odd else error_buf.at[packed]
+        basis_from = odd_basis.at[matrix] if odd else right_buf.at[packed]
+        return (
+            pltpu.make_async_copy(error_from, error_refs[index].at[(0,) + where], sems.at[0, slot]),
+            pltpu.make_async_copy(basis_from, basis_refs[index].at[where], sems.at[1, slot]),
+        )
+
+    def run(half_core, ranges):
+        if stage == 2:
+            for offset, width, part in layout.cells:
+                half = width // 2
+                source = (slice(None), pl.ds(offset // 2, half))
+                values = [ref[source] for ref in right_refs]
+                for number in range(2):
+                    value = jnp.where(named[part] == number, values[0], values[1])
+                    right_buf[:, pl.ds(half_core * layout.half + offset + number * half, half)] = value
+        for slot, chunk in enumerate(update_chunks(layout, ranges)):
+            index, matrix, _, place, width, source = chunk
+            padded = round_up(width, LANES)
+            packed = (slice(None), pl.ds(place, padded))
+            if stage == 2:
+                right = right_buf[packed]
+            else:
+                right = right_refs[0][:, pl.ds(source, padded)]
+                right_buf[packed] = right
+            high, low = split2(right)
+            approx = dot_plain(turned_ref[layout.firsts[index] + matrix], jnp.concatenate([high, low, high], axis=0))
+            error = merged_ref[packed] - approx
+            error_buf[packed] = error
+            if width < padded:
+                odd_error[matrix] = error[:, :width]
+                odd_basis[matrix] = right[:, :width]
+            for copy in copies_of(chunk, slot):
+                copy.start()
+        for slot, chunk in enumerate(update_chunks(layout, ranges)):
+            for copy in copies_of(chunk, slot):
+                copy.wait()
+
+    for half_core, bits, ranges in update_regions(layout, stage):
+        if bits is None:
+            mine = core != half_core
+        else:
+            mine = (core == half_core) & (named[0] == bits[0]) & (named[1] == bits[1])
+        pl.when(mine)(functools.partial(run, half_core, ranges))
 
 
 def update_error(layout, rank, stage, turned, merged, rights, before=()):
@@ -485,11 +491,7 @@
         refs = refs[ins + len(before) :]
         update_kernel(layout, stage, turned_ref, merged_ref, right_refs, refs[:groups], refs[groups : 2 * groups], *refs[2 * groups :])
 
-    slots = 0
-    for low in range(0, layout.packed, layout.half):
-        for offset, width, _ in layout.cells:
-            for begin in (low + offset, low + offset + width // 2):
-                slots += sum(segment[-1] for segment in layout.segments(begin, begin + width // 2, 4096))
+    slots = max(len(list(update_chunks(layout, ranges))) for _, _, ranges in update_regions(layout, stage))
     return pl.pallas_call(
         kernel,
         name="update_" + ("first", "own", "other")[stage],

time: 59.7 us -> 59.5 us (level)
  Pallas kernels: 15.9 us -> 15.2 us
  waiting for transfers between devices: 20.3 us -> 20.9 us
    pallas_call x3, Pallas kernels: 6.27 us -> 5.54 us  [update_error(): pl.pallas_call(kernel, name='update_' + ('first', 'own', 'other')[stage],...]
  transfers between devices with their start and end apart: 23 -> 23, of which waited for: 14 -> 14; matrix products, arithmetic and copies ran while one was open for 0% -> 0% of each run, Pallas kernels for 8% -> 7%
where the time goes in v2:
time: 59.5 us; the launch traced here: 59.4 us
  starting transfers between devices  22.5 us (38%)
  waiting for transfers between devices  20.9 us (35%)
  Pallas kernels  15.2 us (26%)
  between operations  0.78 us (1%)
    ppermute x17, starting transfers between devices, swap(): return lax.ppermute(value, axis, [(i, i ^ 1 << bit) for i in range(size)])  13.9 us
    ppermute x17, waiting for transfers between devices, swap(): return lax.ppermute(value, axis, [(i, i ^ 1 << bit) for i in range(size)])  13.1 us
    ppermute x6, starting transfers between devices, sum_over_bits(): lax.ppermute(value, axis, [(i, i ^ turn) for i in range(size)])  8.62 us
    ppermute x6, waiting for transfers between devices, sum_over_bits(): lax.ppermute(value, axis, [(i, i ^ turn) for i in range(size)])  7.79 us
    pallas_call x3, Pallas kernels, update_error(): pl.pallas_call(kernel, name='update_' + ('first', 'own', 'other')[stage],...  5.54 us
    pallas_call x1, Pallas kernels, merge_and_project(): pl.pallas_call(kernel, name='merge_and_project', out_shape=[pltpu.VMEM((r...  5.46 us
    pallas_call x1, Pallas kernels, factor(): pl.pallas_call(functools.partial(factor_kernel, layout), name='factor', o...  3.05 us
  transfers between devices with their start and end apart: 23, of which 14 were waited for; matrix products, arithmetic and copies ran while one was open for 0% of the time, Pallas kernels for 7%

profile of v2, /device:TPU:0, one launch (start us, length us, event | category | flops | bytes accessed | tf_op | source)
XLA Modules:
  0.0 59.4 jit_solution(9012464183010691056)
XLA Ops:
  0.6 5.5 %merge_and_project.1 = (f32[64,20992]{1,0:T(8,128)S(1)}, f32[7,8,128]{2,1,0:T(8,128)S(1)}, f32[7,8,128]{2,1,0:T(8,128)S(1)}) custom-call(bf16[1,3,64,2048]{3,2,1,0:T(8,128)(2,1)} %refs_0_.1, bf16[1,2,64,256]{3,2,1,0:T(8,128)(2,1)} %refs_1_.1, bf16[1,2,64,7168]{3,2,1,0:T(8,128)(2,1)} %refs_2_.1, f32[1,3,64,2048]{3,2,1,0:T(8,128)} %refs_3_.1, ...), custom_call_target="tpu_custom_call" | custom-call | flops 343932928 | bytes 10747904 | tf_op jit(solution)/shard_map/merge_and_project/pallas_call | solution.py:192
  6.1 0.5 collective-permute-start
  6.6 0.9 %collective-permute-done = f32[7,8,128]{2,1,0:T(8,128)S(1)} collective-permute-done((f32[7,8,128]{2,1,0:T(8,128)S(1)}, f32[7,8,128]{2,1,0:T(8,128)S(1)}, u32[]{:S(2)}, u32[]{:S(2)}) %collective-permute-start) | collective-permute-done | bytes 28704 | tf_op jit(solution)/shard_map/ppermute | solution.py:516
  8.1 3.6 %collective-permute-start.4 = (f32[7,8,128]{2,1,0:T(8,128)S(1)}, f32[7,8,128]{2,1,0:T(8,128)S(1)}, u32[]{:S(2)}, u32[]{:S(2)}) collective-permute-start(f32[7,8,128]{2,1,0:T(8,128)S(1)} %add.21), channel_id=1, source_target_pairs={{0,24},{4,28},{8,16},{12,20},{16,8},{20,12},{24,0},{28,4},{1,25},{... | collective-permute-start | bytes 86024 | tf_op jit(solution)/shard_map/ppermute | solution.py:525
  12.2 1.3 %collective-permute-done.4 = f32[7,8,128]{2,1,0:T(8,128)S(1)} collective-permute-done((f32[7,8,128]{2,1,0:T(8,128)S(1)}, f32[7,8,128]{2,1,0:T(8,128)S(1)}, u32[]{:S(2)}, u32[]{:S(2)}) %collective-permute-start.4) | collective-permute-done | bytes 28704 | tf_op jit(solution)/shard_map/ppermute | solution.py:525
  13.5 2.0 %collective-permute-done.3 = f32[7,8,128]{2,1,0:T(8,128)S(1)} collective-permute-done((f32[7,8,128]{2,1,0:T(8,128)S(1)}, f32[7,8,128]{2,1,0:T(8,128)S(1)}, u32[]{:S(2)}, u32[]{:S(2)}) %collective-permute-start.3) | collective-permute-done | bytes 28704 | tf_op jit(solution)/shard_map/ppermute | solution.py:525
  16.1 3.7 %collective-permute-start.7 = (f32[7,8,128]{2,1,0:T(8,128)S(1)}, f32[7,8,128]{2,1,0:T(8,128)S(1)}, u32[]{:S(2)}, u32[]{:S(2)}) collective-permute-start(f32[7,8,128]{2,1,0:T(8,128)S(1)} %add_add_fusion.1), channel_id=1, source_target_pairs={{0,3},{1,2},{2,1},{3,0},{4,7},{5,6},{6,5},{7,4},{8,11},{9,10},{10,... | collective-permute-start | bytes 86024 | tf_op jit(solution)/shard_map/ppermute | solution.py:525
  19.7 0.8 %collective-permute-start.5 = (f32[7,8,128]{2,1,0:T(8,128)S(1)}, f32[7,8,128]{2,1,0:T(8,128)S(1)}, u32[]{:S(2)}, u32[]{:S(2)}) collective-permute-start(f32[7,8,128]{2,1,0:T(8,128)S(1)} %add_add_fusion.1), channel_id=1, source_target_pairs={{0,1},{1,0},{2,3},{3,2},{4,5},{5,4},{6,7},{7,6},{8,9},{9,8},{10,11... | collective-permute-start | bytes 86024 | tf_op jit(solution)/shard_map/ppermute | solution.py:525
  20.5 1.3 %collective-permute-done.7 = f32[7,8,128]{2,1,0:T(8,128)S(1)} collective-permute-done((f32[7,8,128]{2,1,0:T(8,128)S(1)}, f32[7,8,128]{2,1,0:T(8,128)S(1)}, u32[]{:S(2)}, u32[]{:S(2)}) %collective-permute-start.7) | collective-permute-done | bytes 28704 | tf_op jit(solution)/shard_map/ppermute | solution.py:525
  21.8 2.7 %collective-permute-done.6 = f32[7,8,128]{2,1,0:T(8,128)S(1)} collective-permute-done((f32[7,8,128]{2,1,0:T(8,128)S(1)}, f32[7,8,128]{2,1,0:T(8,128)S(1)}, u32[]{:S(2)}, u32[]{:S(2)}) %collective-permute-start.6) | collective-permute-done | bytes 28704 | tf_op jit(solution)/shard_map/ppermute | solution.py:525
  24.6 0.6 split_sum.1.sums_ref
  25.2 0.6 %collective-permute-done.8.other_ref = f32[7,8,128]{2,1,0:T(8,128)S(1)} collective-permute-done((f32[7,8,128]{2,1,0:T(8,128)S(1)}, f32[7,8,128]{2,1,0:T(8,128)S(1)}, u32[]{:S(2)}, u32[]{:S(2)}) %collective-permute-start.8) | collective-permute-done | bytes 28704 | tf_op jit(solution)/shard_map/ppermute | solution.py:516
  25.8 3.1 %factor.1 = (f32[7,32,64]{2,1,0:T(8,128)}, f32[32,1536]{1,0:T(8,128)S(1)}, f32[32,1536]{1,0:T(8,128)S(1)}, f32[32,1536]{1,0:T(8,128)S(1)}, f32[32,1536]{1,0:T(8,...) custom-call(f32[7,8,128]{2,1,0:T(8,128)S(1)} %add_add_fusion.own_ref,, ...), custom_call_target="tpu_custom_call" | custom-call | flops 171966464 | bytes 10000000 | tf_op jit(solution)/shard_map/factor/pallas_call | solution.py:372
  28.8 0.5 collective-permute-start.9
  29.4 1.5 %collective-permute-start.10 = (f32[32,1536]{1,0:T(8,128)S(1)}, f32[32,1536]{1,0:T(8,128)S(1)}, u32[]{:S(2)}, u32[]{:S(2)}) collective-permute-start(f32[32,1536]{1,0:T(8,128)S(1)} %get-tuple-element.72), channel_id=1, source_target_pairs={{0,16},{4,20},{8,24},{12,28},{16,0},{20,4},{24,8},{28,12},{1,17},{... | collective-permute-start | bytes 589832 | tf_op jit(solution)/shard_map/ppermute | solution.py:516
  30.9 1.5 %collective-permute-start.13 = (f32[32,1280]{1,0:T(8,128)S(1)}, f32[32,1280]{1,0:T(8,128)S(1)}, u32[]{:S(2)}, u32[]{:S(2)}) collective-permute-start(f32[32,1280]{1,0:T(8,128)S(1)} %get-tuple-element.78), channel_id=1, source_target_pairs={{0,8},{4,12},{8,0},{12,4},{16,24},{20,28},{24,16},{28,20},{1,9},{5... | collective-permute-start | bytes 491528 | tf_op jit(solution)/shard_map/ppermute | solution.py:516
  32.9 3.7 %collective-permute-done.9.refs_1_ = f32[32,1536]{1,0:T(8,128)S(1)} collective-permute-done((f32[32,1536]{1,0:T(8,128)S(1)}, f32[32,1536]{1,0:T(8,128)S(1)}, u32[]{:S(2)}, u32[]{:S(2)}) %collective-permute-start.9) | collective-permute-done | bytes 196640 | tf_op jit(solution)/shard_map/ppermute | solution.py:516
  36.6 0.6 collective-permute-done.10.refs_3_
  37.2 1.6 %collective-permute-start.11 = (f32[32,1536]{1,0:T(8,128)S(1)}, f32[32,1536]{1,0:T(8,128)S(1)}, u32[]{:S(2)}, u32[]{:S(2)}) collective-permute-start(f32[32,1536]{1,0:T(8,128)S(1)} %get-tuple-element.73.refs_0_), channel_id=1, source_target_pairs={{0,16},{4,20},{8,24},{12,28},{16,0},{20,4},{24,8},{28,12},{1,17},{... | collective-permute-start | bytes 589832 | tf_op jit(solution)/shard_map/ppermute | solution.py:516
  38.8 1.5 %collective-permute-start.12 = (f32[32,1536]{1,0:T(8,128)S(1)}, f32[32,1536]{1,0:T(8,128)S(1)}, u32[]{:S(2)}, u32[]{:S(2)}) collective-permute-start(f32[32,1536]{1,0:T(8,128)S(1)} %get-tuple-element.74.refs_2_), channel_id=1, source_target_pairs={{0,8},{4,12},{8,0},{12,4},{16,24},{20,28},{24,16},{28,20},{1,9},{5... | collective-permute-start | bytes 589832 | tf_op jit(solution)/shard_map/ppermute | solution.py:516
  40.4 1.4 %collective-permute-start.15 = (f32[32,1280]{1,0:T(8,128)S(1)}, f32[32,1280]{1,0:T(8,128)S(1)}, u32[]{:S(2)}, u32[]{:S(2)}) collective-permute-start(f32[32,1280]{1,0:T(8,128)S(1)} %get-tuple-element.81.refs_0_), channel_id=1, source_target_pairs={{0,16},{4,20},{8,24},{12,28},{16,0},{20,4},{24,8},{28,12},{1,17},{... | collective-permute-start | bytes 491528 | tf_op jit(solution)/shard_map/ppermute | solution.py:516
  41.7 0.6 %collective-permute-start.16 = (f32[32,896]{1,0:T(8,128)S(1)}, f32[32,896]{1,0:T(8,128)S(1)}, u32[]{:S(2)}, u32[]{:S(2)}) collective-permute-start(f32[32,896]{1,0:T(8,128)S(1)} %get-tuple-element.82.refs_2_), channel_id=1, source_target_pairs={{0,8},{4,12},{8,0},{12,4},{16,24},{20,28},{24,16},{28,20},{1,9},{5... | collective-permute-start | bytes 344072 | tf_op jit(solution)/shard_map/ppermute | solution.py:516
  42.3 2.3 %collective-permute-done.11.refs_1_ = f32[32,1536]{1,0:T(8,128)S(1)} collective-permute-done((f32[32,1536]{1,0:T(8,128)S(1)}, f32[32,1536]{1,0:T(8,128)S(1)}, u32[]{:S(2)}, u32[]{:S(2)}) %collective-permute-start.11) | collective-permute-done | bytes 196640 | tf_op jit(solution)/shard_map/ppermute | solution.py:516
  44.6 1.7 %collective-permute-done.12.refs_3_ = f32[32,1536]{1,0:T(8,128)S(1)} collective-permute-done((f32[32,1536]{1,0:T(8,128)S(1)}, f32[32,1536]{1,0:T(8,128)S(1)}, u32[]{:S(2)}, u32[]{:S(2)}) %collective-permute-start.12) | collective-permute-done | bytes 196640 | tf_op jit(solution)/shard_map/ppermute | solution.py:516
  46.4 1.2 %collective-permute-start.18 = (f32[32,1536]{1,0:T(8,128)S(1)}, f32[32,1536]{1,0:T(8,128)S(1)}, u32[]{:S(2)}, u32[]{:S(2)}) collective-permute-start(f32[32,1536]{1,0:T(8,128)S(1)} %get-tuple-element.75.refs_0_), channel_id=1, source_target_pairs={{0,8},{4,12},{8,0},{12,4},{16,24},{20,28},{24,16},{28,20},{1,9},{5... | collective-permute-start | bytes 589832 | tf_op jit(solution)/shard_map/ppermute | solution.py:516
  47.8 1.0 %collective-permute-done.16.refs_3_ = f32[32,896]{1,0:T(8,128)S(1)} collective-permute-done((f32[32,896]{1,0:T(8,128)S(1)}, f32[32,896]{1,0:T(8,128)S(1)}, u32[]{:S(2)}, u32[]{:S(2)}) %collective-permute-start.16) | collective-permute-done | bytes 114720 | tf_op jit(solution)/shard_map/ppermute | solution.py:516
  48.8 1.2 %collective-permute-start.20 = (f32[32,1280]{1,0:T(8,128)S(1)}, f32[32,1280]{1,0:T(8,128)S(1)}, u32[]{:S(2)}, u32[]{:S(2)}) collective-permute-start(f32[32,1280]{1,0:T(8,128)S(1)} %get-tuple-element.85.refs_2_), channel_id=1, source_target_pairs={{0,8},{4,12},{8,0},{12,4},{16,24},{20,28},{24,16},{28,20},{1,9},{5... | collective-permute-start | bytes 491528 | tf_op jit(solution)/shard_map/ppermute | solution.py:516
  50.0 1.0 %collective-permute-start.21 = (f32[32,896]{1,0:T(8,128)S(1)}, f32[32,896]{1,0:T(8,128)S(1)}, u32[]{:S(2)}, u32[]{:S(2)}) collective-permute-start(f32[32,896]{1,0:T(8,128)S(1)} %get-tuple-element.86.refs_3_), channel_id=1, source_target_pairs={{0,16},{4,20},{8,24},{12,28},{16,0},{20,4},{24,8},{28,12},{1,17},{... | collective-permute-start | bytes 344072 | tf_op jit(solution)/shard_map/ppermute | solution.py:516
  51.3 1.6 %update_first.1 = (f32[1,3,64,2048]{3,2,1,0:T(8,128)}, f32[1,2,64,256]{3,2,1,0:T(8,128)}, f32[1,2,64,7168]{3,2,1,0:T(8,128)}, f32[3,32,2048]{2,1,0:T(8,128)}, f3...) custom-call(bf16[7,64,96]{2,1,0:T(8,128)(2,1)S(1)} %turn.1.refs_0_, f32[64,20992]{1,0:T(8,128)S(1)} %get-tuple-element.64.merged_ref.refs_1_, ...), custom_call_target="tpu_custom_call" | custom-call | flops 100000 | bytes 100000 | tf_op jit(solution)/shard_map/update_first/pallas_call | solution.py:495
  52.9 1.9 %collective-permute-done.21.refs_3_ = f32[32,896]{1,0:T(8,128)S(1)} collective-permute-done((f32[32,896]{1,0:T(8,128)S(1)}, f32[32,896]{1,0:T(8,128)S(1)}, u32[]{:S(2)}, u32[]{:S(2)}) %collective-permute-start.21) | collective-permute-done | bytes 114720 | tf_op jit(solution)/shard_map/ppermute | solution.py:516
  54.9 1.6 %update_own.1 = (f32[1,3,64,2048]{3,2,1,0:T(8,128)}, f32[1,2,64,256]{3,2,1,0:T(8,128)}, f32[1,2,64,7168]{3,2,1,0:T(8,128)}, f32[3,32,2048]{2,1,0:T(8,128)}, f32[...) custom-call(bf16[7,64,96]{2,1,0:T(8,128)(2,1)S(1)} %turn.1.refs_0_, ...), custom_call_target="tpu_custom_call", output_to_operand_aliasing={{0}: (3, {}), {1}: (4, {}), {2}: (5, {}), {3}: (6, {}), {4}... | custom-call | flops 100000 | bytes 40000000 | tf_op jit(solution)/shard_map/update_own/pallas_call | solution.py:495
  57.0 2.4 %update_other.1 = (f32[1,3,64,2048]{3,2,1,0:T(8,128)}, f32[1,2,64,256]{3,2,1,0:T(8,128)}, f32[1,2,64,7168]{3,2,1,0:T(8,128)}, f32[3,32,2048]{2,1,0:T(8,128)}, f3...) custom-call(bf16[7,64,96]{2,1,0:T(8,128)(2,1)S(1)} %turn.1.refs_0_, ...), custom_call_target="tpu_custom_call", output_to_operand_aliasing={{0}: (4, {}), {1}: (5, {}), {2}: (6, {}), {3}: (7, {}), {4}... | custom-call | flops 100000 | bytes 40000000 | tf_op jit(solution)/shard_map/update_other/pallas_call | solution.py:495
  (33 shorter events, 3.6 us)
Async XLA Ops:
  6.1 1.4 %collective-permute-start = (f32[7,8,128]{2,1,0:T(8,128)S(1)}, f32[7,8,128]{2,1,0:T(8,128)S(1)}, u32[]{:S(2)}, u32[]{:S(2)}) collective-permute-start(f32[7,8,128]{2,1,0:T(8,128)S(1)} %get-tuple-element.63), channel_id=1, source_target_pairs={{0,4},{4,0},{8,12},{12,8},{16,20},{20,16},{24,28},{28,24},{1,5},{5... | collective-permute-start | bytes 86024 | tf_op jit(solution)/shard_map/ppermute | solution.py:516
  7.7 16.9 %collective-permute-start.1 = (f32[64,10496]{1,0:T(8,128)S(1)}, f32[64,10496]{1,0:T(8,128)S(1)}, u32[]{:S(2)}, u32[]{:S(2)}) collective-permute-start(f32[64,10496]{1,0:T(8,128)S(1)} %take_half.1), channel_id=1, source_target_pairs={{0,4},{4,0},{8,12},{12,8},{16,20},{20,16},{24,28},{28,24},{1,5},{5... | collective-permute-start | bytes 8060936 | tf_op jit(solution)/shard_map/ppermute | solution.py:516
  8.1 5.5 %collective-permute-start.4 = (f32[7,8,128]{2,1,0:T(8,128)S(1)}, f32[7,8,128]{2,1,0:T(8,128)S(1)}, u32[]{:S(2)}, u32[]{:S(2)}) collective-permute-start(f32[7,8,128]{2,1,0:T(8,128)S(1)} %add.21), channel_id=1, source_target_pairs={{0,24},{4,28},{8,16},{12,20},{16,8},{20,12},{24,0},{28,4},{1,25},{... | collective-permute-start | bytes 86024 | tf_op jit(solution)/shard_map/ppermute | solution.py:525
  11.7 3.9 %collective-permute-start.3 = (f32[7,8,128]{2,1,0:T(8,128)S(1)}, f32[7,8,128]{2,1,0:T(8,128)S(1)}, u32[]{:S(2)}, u32[]{:S(2)}) collective-permute-start(f32[7,8,128]{2,1,0:T(8,128)S(1)} %add.21), channel_id=1, source_target_pairs={{0,16},{4,20},{8,24},{12,28},{16,0},{20,4},{24,8},{28,12},{1,17},{... | collective-permute-start | bytes 86024 | tf_op jit(solution)/shard_map/ppermute | solution.py:525
  12.2 3.9 %collective-permute-start.2 = (f32[7,8,128]{2,1,0:T(8,128)S(1)}, f32[7,8,128]{2,1,0:T(8,128)S(1)}, u32[]{:S(2)}, u32[]{:S(2)}) collective-permute-start(f32[7,8,128]{2,1,0:T(8,128)S(1)} %add.21), channel_id=1, source_target_pairs={{0,8},{4,12},{8,0},{12,4},{16,24},{20,28},{24,16},{28,20},{1,9},{5... | collective-permute-start | bytes 86024 | tf_op jit(solution)/shard_map/ppermute | solution.py:525
  16.1 5.8 %collective-permute-start.7 = (f32[7,8,128]{2,1,0:T(8,128)S(1)}, f32[7,8,128]{2,1,0:T(8,128)S(1)}, u32[]{:S(2)}, u32[]{:S(2)}) collective-permute-start(f32[7,8,128]{2,1,0:T(8,128)S(1)} %add_add_fusion.1), channel_id=1, source_target_pairs={{0,3},{1,2},{2,1},{3,0},{4,7},{5,6},{6,5},{7,4},{8,11},{9,10},{10,... | collective-permute-start | bytes 86024 | tf_op jit(solution)/shard_map/ppermute | solution.py:525
  19.7 4.8 %collective-permute-start.6 = (f32[7,8,128]{2,1,0:T(8,128)S(1)}, f32[7,8,128]{2,1,0:T(8,128)S(1)}, u32[]{:S(2)}, u32[]{:S(2)}) collective-permute-start(f32[7,8,128]{2,1,0:T(8,128)S(1)} %add_add_fusion.1), channel_id=1, source_target_pairs={{0,2},{1,3},{2,0},{3,1},{4,6},{5,7},{6,4},{7,5},{8,10},{9,11},{10,... | collective-permute-start | bytes 86024 | tf_op jit(solution)/shard_map/ppermute | solution.py:525
  19.7 4.8 %collective-permute-start.5 = (f32[7,8,128]{2,1,0:T(8,128)S(1)}, f32[7,8,128]{2,1,0:T(8,128)S(1)}, u32[]{:S(2)}, u32[]{:S(2)}) collective-permute-start(f32[7,8,128]{2,1,0:T(8,128)S(1)} %add_add_fusion.1), channel_id=1, source_target_pairs={{0,1},{1,0},{2,3},{3,2},{4,5},{5,4},{6,7},{7,6},{8,9},{9,8},{10,11... | collective-permute-start | bytes 86024 | tf_op jit(solution)/shard_map/ppermute | solution.py:525
  24.5 1.3 %collective-permute-start.8 = (f32[7,8,128]{2,1,0:T(8,128)S(1)}, f32[7,8,128]{2,1,0:T(8,128)S(1)}, u32[]{:S(2)}, u32[]{:S(2)}) collective-permute-start(f32[7,8,128]{2,1,0:T(8,128)S(1)} %add_add_fusion.own_ref), channel_id=1, source_target_pairs={{0,4},{4,0},{8,12},{12,8},{16,20},{20,16},{24,28},{28,24},{1,5},{5... | collective-permute-start | bytes 86024 | tf_op jit(solution)/shard_map/ppermute | solution.py:516
  28.8 22.2 %copy-start = (f32[7,32,64]{2,1,0:T(8,128)S(1)}, f32[7,32,64]{2,1,0:T(8,128)}, u32[]{:S(2)}) copy-start(f32[7,32,64]{2,1,0:T(8,128)} %get-tuple-element.68.left_ref) | copy-start | bytes 172036
  28.8 7.7 %collective-permute-start.9 = (f32[32,1536]{1,0:T(8,128)S(1)}, f32[32,1536]{1,0:T(8,128)S(1)}, u32[]{:S(2)}, u32[]{:S(2)}) collective-permute-start(f32[32,1536]{1,0:T(8,128)S(1)} %get-tuple-element.70), channel_id=1, source_target_pairs={{0,8},{4,12},{8,0},{12,4},{16,24},{20,28},{24,16},{28,20},{1,9},{5... | collective-permute-start | bytes 589832 | tf_op jit(solution)/shard_map/ppermute | solution.py:516
  29.4 7.8 %collective-permute-start.10 = (f32[32,1536]{1,0:T(8,128)S(1)}, f32[32,1536]{1,0:T(8,128)S(1)}, u32[]{:S(2)}, u32[]{:S(2)}) collective-permute-start(f32[32,1536]{1,0:T(8,128)S(1)} %get-tuple-element.72), channel_id=1, source_target_pairs={{0,16},{4,20},{8,24},{12,28},{16,0},{20,4},{24,8},{28,12},{1,17},{... | collective-permute-start | bytes 589832 | tf_op jit(solution)/shard_map/ppermute | solution.py:516
  30.9 9.4 %collective-permute-start.13 = (f32[32,1280]{1,0:T(8,128)S(1)}, f32[32,1280]{1,0:T(8,128)S(1)}, u32[]{:S(2)}, u32[]{:S(2)}) collective-permute-start(f32[32,1280]{1,0:T(8,128)S(1)} %get-tuple-element.78), channel_id=1, source_target_pairs={{0,8},{4,12},{8,0},{12,4},{16,24},{20,28},{24,16},{28,20},{1,9},{5... | collective-permute-start | bytes 491528 | tf_op jit(solution)/shard_map/ppermute | solution.py:516
  32.4 7.9 %collective-permute-start.14 = (f32[32,896]{1,0:T(8,128)S(1)}, f32[32,896]{1,0:T(8,128)S(1)}, u32[]{:S(2)}, u32[]{:S(2)}) collective-permute-start(f32[32,896]{1,0:T(8,128)S(1)} %get-tuple-element.80), channel_id=1, source_target_pairs={{0,16},{4,20},{8,24},{12,28},{16,0},{20,4},{24,8},{28,12},{1,17},{... | collective-permute-start | bytes 344072 | tf_op jit(solution)/shard_map/ppermute | solution.py:516
  37.2 7.4 %collective-permute-start.11 = (f32[32,1536]{1,0:T(8,128)S(1)}, f32[32,1536]{1,0:T(8,128)S(1)}, u32[]{:S(2)}, u32[]{:S(2)}) collective-permute-start(f32[32,1536]{1,0:T(8,128)S(1)} %get-tuple-element.73.refs_0_), channel_id=1, source_target_pairs={{0,16},{4,20},{8,24},{12,28},{16,0},{20,4},{24,8},{28,12},{1,17},{... | collective-permute-start | bytes 589832 | tf_op jit(solution)/shard_map/ppermute | solution.py:516
  38.8 7.5 %collective-permute-start.12 = (f32[32,1536]{1,0:T(8,128)S(1)}, f32[32,1536]{1,0:T(8,128)S(1)}, u32[]{:S(2)}, u32[]{:S(2)}) collective-permute-start(f32[32,1536]{1,0:T(8,128)S(1)} %get-tuple-element.74.refs_2_), channel_id=1, source_target_pairs={{0,8},{4,12},{8,0},{12,4},{16,24},{20,28},{24,16},{28,20},{1,9},{5... | collective-permute-start | bytes 589832 | tf_op jit(solution)/shard_map/ppermute | solution.py:516
  40.4 8.4 %collective-permute-start.15 = (f32[32,1280]{1,0:T(8,128)S(1)}, f32[32,1280]{1,0:T(8,128)S(1)}, u32[]{:S(2)}, u32[]{:S(2)}) collective-permute-start(f32[32,1280]{1,0:T(8,128)S(1)} %get-tuple-element.81.refs_0_), channel_id=1, source_target_pairs={{0,16},{4,20},{8,24},{12,28},{16,0},{20,4},{24,8},{28,12},{1,17},{... | collective-permute-start | bytes 491528 | tf_op jit(solution)/shard_map/ppermute | solution.py:516
  41.7 7.1 %collective-permute-start.16 = (f32[32,896]{1,0:T(8,128)S(1)}, f32[32,896]{1,0:T(8,128)S(1)}, u32[]{:S(2)}, u32[]{:S(2)}) collective-permute-start(f32[32,896]{1,0:T(8,128)S(1)} %get-tuple-element.82.refs_2_), channel_id=1, source_target_pairs={{0,8},{4,12},{8,0},{12,4},{16,24},{20,28},{24,16},{28,20},{1,9},{5... | collective-permute-start | bytes 344072 | tf_op jit(solution)/shard_map/ppermute | solution.py:516
  46.4 8.4 %collective-permute-start.18 = (f32[32,1536]{1,0:T(8,128)S(1)}, f32[32,1536]{1,0:T(8,128)S(1)}, u32[]{:S(2)}, u32[]{:S(2)}) collective-permute-start(f32[32,1536]{1,0:T(8,128)S(1)} %get-tuple-element.75.refs_0_), channel_id=1, source_target_pairs={{0,8},{4,12},{8,0},{12,4},{16,24},{20,28},{24,16},{28,20},{1,9},{5... | collective-permute-start | bytes 589832 | tf_op jit(solution)/shard_map/ppermute | solution.py:516
  47.5 7.3 %collective-permute-start.19 = (f32[32,1536]{1,0:T(8,128)S(1)}, f32[32,1536]{1,0:T(8,128)S(1)}, u32[]{:S(2)}, u32[]{:S(2)}) collective-permute-start(f32[32,1536]{1,0:T(8,128)S(1)} %get-tuple-element.76.refs_1_), channel_id=1, source_target_pairs={{0,16},{4,20},{8,24},{12,28},{16,0},{20,4},{24,8},{28,12},{1,17},{... | collective-permute-start | bytes 589832 | tf_op jit(solution)/shard_map/ppermute | solution.py:516
  48.8 6.0 %collective-permute-start.20 = (f32[32,1280]{1,0:T(8,128)S(1)}, f32[32,1280]{1,0:T(8,128)S(1)}, u32[]{:S(2)}, u32[]{:S(2)}) collective-permute-start(f32[32,1280]{1,0:T(8,128)S(1)} %get-tuple-element.85.refs_2_), channel_id=1, source_target_pairs={{0,8},{4,12},{8,0},{12,4},{16,24},{20,28},{24,16},{28,20},{1,9},{5... | collective-permute-start | bytes 491528 | tf_op jit(solution)/shard_map/ppermute | solution.py:516
  50.0 4.8 %collective-permute-start.21 = (f32[32,896]{1,0:T(8,128)S(1)}, f32[32,896]{1,0:T(8,128)S(1)}, u32[]{:S(2)}, u32[]{:S(2)}) collective-permute-start(f32[32,896]{1,0:T(8,128)S(1)} %get-tuple-element.86.refs_3_), channel_id=1, source_target_pairs={{0,16},{4,20},{8,24},{12,28},{16,0},{20,4},{24,8},{28,12},{1,17},{... | collective-permute-start | bytes 344072 | tf_op jit(solution)/shard_map/ppermute | solution.py:516
  51.2 5.3 %collective-permute-start.17 = (f32[32,5248]{1,0:T(8,128)S(1)}, f32[32,5248]{1,0:T(8,128)S(1)}, u32[]{:S(2)}, u32[]{:S(2)}) collective-permute-start(f32[32,5248]{1,0:T(8,128)S(1)} %pack.2.refs_2_), channel_id=1, source_target_pairs={{0,4},{4,0},{8,12},{12,8},{16,20},{20,16},{24,28},{28,24},{1,5},{5... | collective-permute-start | bytes 2015240 | tf_op jit(solution)/shard_map/ppermute | solution.py:516
  54.9 2.2 %collective-permute-start.22 = (f32[32,5248]{1,0:T(8,128)S(1)}, f32[32,5248]{1,0:T(8,128)S(1)}, u32[]{:S(2)}, u32[]{:S(2)}) collective-permute-start(f32[32,5248]{1,0:T(8,128)S(1)} %pack.3.refs_2_), channel_id=1, source_target_pairs={{0,4},{4,0},{8,12},{12,8},{16,20},{20,16},{24,28},{28,24},{1,5},{5... | collective-permute-start | bytes 2015240 | tf_op jit(solution)/shard_map/ppermute | solution.py:516

commit v3 on v2

--- a/solution.py
+++ b/solution.py
@@ -313,7 +313,8 @@
             for j in range(matrices)
         ]
     )
-    filler = jnp.zeros((matrices, rank, LANES - rank - rows), F32)
+    spare = (matrices, rank, LANES - rank - rows)
+    filler = (lax.broadcasted_iota(jnp.int32, spare, 1) == lax.broadcasted_iota(jnp.int32, spare, 2)).astype(F32)
     work = jnp.concatenate([gram, filler, product_t], axis=2)
     done = []
     for first in range(0, rank, block):
@@ -342,18 +343,19 @@
     row_id = lax.broadcasted_iota(jnp.int32, work.shape, 1)
     lane_id = lax.broadcasted_iota(jnp.int32, work.shape, 2)
     pivots = jnp.sum(jnp.where(row_id == lane_id, work, 0.0), axis=2, keepdims=True)
-    return work[:, :, LANES - rows :] * (1.0 / jnp.sqrt(pivots))
-
-
-def factor_kernel(layout, own_ref, other_ref, sums_ref, left_ref, *refs):
+    scale = 1.0 / jnp.sqrt(pivots)
+    return work[:, :, LANES - rows :] * scale, work[:, :, rank : 2 * rank] * scale
+
+
+def project_back_kernel(layout, own_ref, other_ref, sums_ref, product_ref, *refs):
     outs, parts_ref = refs[:-1], refs[-1]
-    rows = left_ref.shape[2]
+    rows = product_ref.shape[2]
     core = bit_of(0)
     own, other = (jnp.concatenate([ref[:, :, :rows], ref[:, :, rows:]], axis=1) for ref in (own_ref, other_ref))
     both = [jnp.where(core == 0, one, two) for one, two in ((own, other), (other, own))]
-    left = orthonormal_rows(jnp.concatenate(both, axis=1))
-    left_ref[...] = left
-    high, low = split2(left)
+    product = jnp.concatenate(both, axis=1)
+    product_ref[...] = product
+    high, low = split2(product)
     parts_ref[...] = jnp.concatenate([high, high, low], axis=2)
     for cell, (offset, width, part) in enumerate(layout.cells):
         which = bit_of(layout.orders[part][0])
@@ -368,11 +370,11 @@
                 out_ref[:, at : at + layout.granule(cell)] = dot_plain(parts_ref[matrix], stacked)
 
 
-def factor(layout, rank, rows, own, other, sums):
+def project_back(layout, rank, rows, own, other, sums):
     return pl.pallas_call(
-        functools.partial(factor_kernel, layout),
-        name="factor",
-        out_shape=[jax.ShapeDtypeStruct((layout.matrices, rank, rows), F32)]
+        functools.partial(project_back_kernel, layout),
+        name="project_back",
+        out_shape=[pltpu.VMEM((layout.matrices, rank, rows), F32)]
         + [jax.ShapeDtypeStruct((rank, width // 2), F32) for _, width, _ in layout.cells for _ in range(2)],
         in_specs=[VMEM_SPEC] * 3,
         out_specs=[VMEM_SPEC] * (1 + 2 * len(layout.cells)),
@@ -382,47 +384,71 @@
     )(own, other, sums)
 
 
-def turn(left):
-    matrices, rank, rows = left.shape
-
-    def kernel(left_ref, out_ref):
-        high, low = split2(left_ref[...])
+def factor(product):
+    matrices, rank, rows = product.shape
+
+    def kernel(product_ref, left_ref, inverse_ref, turned_ref):
+        left, inverse = orthonormal_rows(product_ref[...])
+        left_ref[...] = left
+        high, low = split2(inverse)
+        inverse_ref[...] = jnp.concatenate([high, high, low], axis=2)
+        high, low = split2(left)
         for j in range(matrices):
-            parts = jnp.concatenate([high[j], high[j], low[j]], axis=0).astype(F32)
-            out_ref[j] = parts.T.astype(BF16)
+            turned_ref[j] = jnp.concatenate([high[j], high[j], low[j]], axis=0).astype(F32).T.astype(BF16)
 
     return pl.pallas_call(
         kernel,
-        name="turn",
-        out_shape=pltpu.VMEM((matrices, rows, 3 * rank), BF16),
+        name="factor",
+        out_shape=[
+            jax.ShapeDtypeStruct((matrices, rank, rows), F32),
+            pltpu.VMEM((matrices, rank, 3 * rank), BF16),
+            pltpu.VMEM((matrices, rows, 3 * rank), BF16),
+        ],
         in_specs=[VMEM_SPEC],
-        out_specs=VMEM_SPEC,
+        out_specs=[VMEM_SPEC] * 3,
         compiler_params=params(),
         cost_estimate=pl.CostEstimate(flops=100_000, bytes_accessed=100_000, transcendentals=0),
-    )(left)
+    )(product)
+
+
+def finish(layout, chunk, halvings, inverse, arrays):
+    def kernel(inverse_ref, *refs):
+        for part in range(2):
+            kept_ref, received_ref = refs[2 * part : 2 * part + 2]
+            cell = 2 * chunk + part
+            offset, width, _ = layout.cells[cell]
+            first = bit_of(0) * layout.half + offset
+            for bit in layout.orders[part][:halvings]:
+                width //= 2
+                first = first + bit_of(bit) * width
+            granule = math.gcd(layout.granule(cell), width)
+            for at in range(0, width, granule):
+                matrix = sum((first + at >= start).astype(jnp.int32) for start in layout.starts[1:])
+                where = (slice(None), slice(at, at + granule))
+                high, low = split2(kept_ref[where] + received_ref[where])
+                refs[4 + part][where] = dot_plain(inverse_ref[matrix], jnp.concatenate([high, low, high], axis=0))
+
+    return add_call("finish", kernel, [arrays[0].shape, arrays[2].shape], (inverse, *arrays))
 
 
 def update_regions(layout, stage):
     regions = []
     for half_core in range(2):
-        origin = half_core * layout.half
-        if stage == 2:
-            regions.append((half_core, None, [(origin, origin + layout.half, None)]))
-            continue
         for bits in ((0, 0), (0, 1), (1, 0), (1, 1)):
             ranges = []
-            for offset, width, part in layout.cells:
-                low = origin + offset + (bits[part] ^ stage) * (width // 2)
-                ranges.append((low, low + width // 2, offset // 2))
+            for owner, flip, source in (((0, 0, 0),), ((0, 1, 0), (1, 0, 1)), ((1, 1, 0),))[stage]:
+                for offset, width, part in layout.cells:
+                    low = (half_core ^ owner) * layout.half + offset + (bits[part] ^ flip) * (width // 2)
+                    ranges.append((low, low + width // 2, offset // 2, source))
             regions.append((half_core, bits, ranges))
     return regions
 
 
 def update_chunks(layout, ranges):
-    for low, high, begin in ranges:
+    for low, high, begin, which in ranges:
         for index, matrix, column, place, width, steps in layout.segments(low, high, 2048):
             for at in range(steps):
-                source = None if begin is None else begin + place - low + at * width
+                source = (which, begin + place - low + at * width)
                 yield index, matrix, column + at * width, place + at * width, width, source
 
 
@@ -443,23 +469,12 @@
         )
 
     def run(half_core, ranges):
-        if stage == 2:
-            for offset, width, part in layout.cells:
-                half = width // 2
-                source = (slice(None), pl.ds(offset // 2, half))
-                values = [ref[source] for ref in right_refs]
-                for number in range(2):
-                    value = jnp.where(named[part] == number, values[0], values[1])
-                    right_buf[:, pl.ds(half_core * layout.half + offset + number * half, half)] = value
         for slot, chunk in enumerate(update_chunks(layout, ranges)):
             index, matrix, _, place, width, source = chunk
             padded = round_up(width, LANES)
             packed = (slice(None), pl.ds(place, padded))
-            if stage == 2:
-                right = right_buf[packed]
-            else:
-                right = right_refs[0][:, pl.ds(source, padded)]
-                right_buf[packed] = right
+            right = right_refs[source[0]][:, pl.ds(source[1], padded)]
+            right_buf[packed] = right
             high, low = split2(right)
             approx = dot_plain(turned_ref[layout.firsts[index] + matrix], jnp.concatenate([high, low, high], axis=0))
             error = merged_ref[packed] - approx
@@ -474,10 +489,7 @@
                 copy.wait()
 
     for half_core, bits, ranges in update_regions(layout, stage):
-        if bits is None:
-            mine = core != half_core
-        else:
-            mine = (core == half_core) & (named[0] == bits[0]) & (named[1] == bits[1])
+        mine = (core == half_core) & (named[0] == bits[0]) & (named[1] == bits[1])
         pl.when(mine)(functools.partial(run, half_core, ranges))
 
 
@@ -553,8 +565,8 @@
     product = sum_over_bits(product, "mp", mp, list(range(mp_bits)))
     received, product = order((received, product))
     sums = split_sum(layout, merged, received)
-    left, *arrays = factor(layout, rank, rows, product, swap(product, "dp", dp, 0), sums)
-    turned = turn(left)
+    product, *arrays = project_back(layout, rank, rows, product, swap(product, "dp", dp, 0), sums)
+    left, inverse, turned = factor(product)
 
     chunks = [arrays[4 * chunk : 4 * chunk + 4] for chunk in range(2)]
     for step in range(max(1, steps - 1)):
@@ -562,12 +574,14 @@
         chunks = [[chunk[1], one, chunk[3], two] for chunk, (one, two) in zip(chunks, traded)]
         if step < steps - 2:
             chunks = [next_sum(layout, step + 1, chunk) for chunk in chunks]
-    chunks = [last_sum(chunk) for chunk in chunks]
-    if steps > 1:
+    if steps == 1:
+        chunks = [finish(layout, number, 1, inverse, chunk) for number, chunk in enumerate(chunks)]
+    else:
+        chunks = [last_sum(chunk) for chunk in chunks]
         traded = [swap_parts(chunk, steps - 1) for chunk in chunks]
-        first = last_sum([chunks[0][0], traded[0][0], chunks[0][1], traded[0][1]])
+        first = finish(layout, 0, steps - 1, inverse, [chunks[0][0], traded[0][0], chunks[0][1], traded[0][1]])
         one, two = order((*traded[1], *first))[:2]
-        chunks = [first, last_sum([chunks[1][0], one, chunks[1][1], two])]
+        chunks = [first, finish(layout, 1, steps - 1, inverse, [chunks[1][0], one, chunks[1][1], two])]
     for step in reversed(range(1, steps - 1)):
         chunks = [join(layout, step, chunk, swap_parts(chunk, step)) for chunk in chunks]
     news = [swap_parts(chunk, 0) for chunk in chunks]
@@ -577,8 +591,8 @@
     tied = order((*outs, *news[0], *news[1]))
     outs, own = tied[: len(outs)], pack(tied[len(outs) :])
     other = swap(own, "dp", dp, 0)
-    outs = update_error(layout, rank, 1, turned, merged, [own], outs)
-    outs = update_error(layout, rank, 2, turned, merged, [first_other, other], outs)
+    outs = update_error(layout, rank, 1, turned, merged, [own, first_other], outs)
+    outs = update_error(layout, rank, 2, turned, merged, [other], outs)
     return (*outs[:3], *(jnp.swapaxes(value, 1, 2) for value in outs[3:]), jnp.swapaxes(left, 1, 2))
 
 

time: 59.5 us -> 57.2 us (0.961)
  waiting for transfers between devices: 20.9 us -> 17.2 us
  starting transfers between devices: 22.5 us -> 23.1 us
    ppermute x17, waiting for transfers between devices: 13.1 us -> 9.43 us  [swap(): return lax.ppermute(value, axis, [(i, i ^ 1 << bit) for i in range(size)])]
  transfers between devices with their start and end apart: 23 -> 23, of which waited for: 14 -> 13; matrix products, arithmetic and copies ran while one was open for 0% -> 0% of each run, Pallas kernels for 7% -> 13%
where the time goes in v3:
time: 57.2 us; the launch traced here: 57 us
  starting transfers between devices  23.1 us (40%)
  waiting for transfers between devices  17.2 us (30%)
  Pallas kernels  15.7 us (27%)
  between operations  0.93 us (2%)
    ppermute x17, starting transfers between devices, swap(): return lax.ppermute(value, axis, [(i, i ^ 1 << bit) for i in range(size)])  14.5 us
    ppermute x17, waiting for transfers between devices, swap(): return lax.ppermute(value, axis, [(i, i ^ 1 << bit) for i in range(size)])  9.43 us
    ppermute x6, starting transfers between devices, sum_over_bits(): lax.ppermute(value, axis, [(i, i ^ turn) for i in range(size)])  8.62 us
    ppermute x6, waiting for transfers between devices, sum_over_bits(): lax.ppermute(value, axis, [(i, i ^ turn) for i in range(size)])  7.8 us
    pallas_call x3, Pallas kernels, update_error(): pl.pallas_call(kernel, name='update_' + ('first', 'own', 'other')[stage],...  5.53 us
    pallas_call x1, Pallas kernels, merge_and_project(): pl.pallas_call(kernel, name='merge_and_project', out_shape=[pltpu.VMEM((r...  5.46 us
    pallas_call x1, Pallas kernels, factor(): pl.pallas_call(kernel, name='factor', out_shape=[jax.ShapeDtypeStruct((ma...  2.3 us
  transfers between devices with their start and end apart: 23, of which 13 were waited for; matrix products, arithmetic and copies ran while one was open for 0% of the time, Pallas kernels for 13%

profile of v3, /device:TPU:0, one launch (start us, length us, event | category | flops | bytes accessed | tf_op | source)
XLA Modules:
  0.0 57.0 jit_solution(8239949584060941581)
XLA Ops:
  0.6 5.5 %merge_and_project.1 = (f32[64,20992]{1,0:T(8,128)S(1)}, f32[7,8,128]{2,1,0:T(8,128)S(1)}, f32[7,8,128]{2,1,0:T(8,128)S(1)}) custom-call(bf16[1,3,64,2048]{3,2,1,0:T(8,128)(2,1)} %refs_0_.1, bf16[1,2,64,256]{3,2,1,0:T(8,128)(2,1)} %refs_1_.1, bf16[1,2,64,7168]{3,2,1,0:T(8,128)(2,1)} %refs_2_.1, f32[1,3,64,2048]{3,2,1,0:T(8,128)} %refs_3_.1, ...), custom_call_target="tpu_custom_call" | custom-call | flops 343932928 | bytes 10747904 | tf_op jit(solution)/shard_map/merge_and_project/pallas_call | solution.py:192
  6.6 0.9 %collective-permute-done = f32[7,8,128]{2,1,0:T(8,128)S(1)} collective-permute-done((f32[7,8,128]{2,1,0:T(8,128)S(1)}, f32[7,8,128]{2,1,0:T(8,128)S(1)}, u32[]{:S(2)}, u32[]{:S(2)}) %collective-permute-start) | collective-permute-done | bytes 28704 | tf_op jit(solution)/shard_map/ppermute | solution.py:528
  8.1 3.6 %collective-permute-start.4 = (f32[7,8,128]{2,1,0:T(8,128)S(1)}, f32[7,8,128]{2,1,0:T(8,128)S(1)}, u32[]{:S(2)}, u32[]{:S(2)}) collective-permute-start(f32[7,8,128]{2,1,0:T(8,128)S(1)} %add.21), channel_id=1, source_target_pairs={{0,24},{4,28},{8,16},{12,20},{16,8},{20,12},{24,0},{28,4},{1,25},{... | collective-permute-start | bytes 86024 | tf_op jit(solution)/shard_map/ppermute | solution.py:537
  12.2 1.3 %collective-permute-done.4 = f32[7,8,128]{2,1,0:T(8,128)S(1)} collective-permute-done((f32[7,8,128]{2,1,0:T(8,128)S(1)}, f32[7,8,128]{2,1,0:T(8,128)S(1)}, u32[]{:S(2)}, u32[]{:S(2)}) %collective-permute-start.4) | collective-permute-done | bytes 28704 | tf_op jit(solution)/shard_map/ppermute | solution.py:537
  13.5 2.0 %collective-permute-done.3 = f32[7,8,128]{2,1,0:T(8,128)S(1)} collective-permute-done((f32[7,8,128]{2,1,0:T(8,128)S(1)}, f32[7,8,128]{2,1,0:T(8,128)S(1)}, u32[]{:S(2)}, u32[]{:S(2)}) %collective-permute-start.3) | collective-permute-done | bytes 28704 | tf_op jit(solution)/shard_map/ppermute | solution.py:537
  16.1 3.7 %collective-permute-start.7 = (f32[7,8,128]{2,1,0:T(8,128)S(1)}, f32[7,8,128]{2,1,0:T(8,128)S(1)}, u32[]{:S(2)}, u32[]{:S(2)}) collective-permute-start(f32[7,8,128]{2,1,0:T(8,128)S(1)} %add_add_fusion.1), channel_id=1, source_target_pairs={{0,3},{1,2},{2,1},{3,0},{4,7},{5,6},{6,5},{7,4},{8,11},{9,10},{10,... | collective-permute-start | bytes 86024 | tf_op jit(solution)/shard_map/ppermute | solution.py:537
  19.7 0.8 %collective-permute-start.5 = (f32[7,8,128]{2,1,0:T(8,128)S(1)}, f32[7,8,128]{2,1,0:T(8,128)S(1)}, u32[]{:S(2)}, u32[]{:S(2)}) collective-permute-start(f32[7,8,128]{2,1,0:T(8,128)S(1)} %add_add_fusion.1), channel_id=1, source_target_pairs={{0,1},{1,0},{2,3},{3,2},{4,5},{5,4},{6,7},{7,6},{8,9},{9,8},{10,11... | collective-permute-start | bytes 86024 | tf_op jit(solution)/shard_map/ppermute | solution.py:537
  20.5 1.3 %collective-permute-done.7 = f32[7,8,128]{2,1,0:T(8,128)S(1)} collective-permute-done((f32[7,8,128]{2,1,0:T(8,128)S(1)}, f32[7,8,128]{2,1,0:T(8,128)S(1)}, u32[]{:S(2)}, u32[]{:S(2)}) %collective-permute-start.7) | collective-permute-done | bytes 28704 | tf_op jit(solution)/shard_map/ppermute | solution.py:537
  21.8 2.7 %collective-permute-done.6 = f32[7,8,128]{2,1,0:T(8,128)S(1)} collective-permute-done((f32[7,8,128]{2,1,0:T(8,128)S(1)}, f32[7,8,128]{2,1,0:T(8,128)S(1)}, u32[]{:S(2)}, u32[]{:S(2)}) %collective-permute-start.6) | collective-permute-done | bytes 28704 | tf_op jit(solution)/shard_map/ppermute | solution.py:537
  24.6 0.6 split_sum.1.sums_ref
  25.2 0.6 %collective-permute-done.8.other_ref = f32[7,8,128]{2,1,0:T(8,128)S(1)} collective-permute-done((f32[7,8,128]{2,1,0:T(8,128)S(1)}, f32[7,8,128]{2,1,0:T(8,128)S(1)}, u32[]{:S(2)}, u32[]{:S(2)}) %collective-permute-start.8) | collective-permute-done | bytes 28704 | tf_op jit(solution)/shard_map/ppermute | solution.py:528
  25.8 1.1 %project_back.1 = (f32[7,32,64]{2,1,0:T(8,128)S(1)}, f32[32,1536]{1,0:T(8,128)S(1)}, f32[32,1536]{1,0:T(8,128)S(1)}, f32[32,1536]{1,0:T(8,128)S(1)}, f32[32,1536...) custom-call(f32[7,8,128]{2,1,0:T(8,128)S(1)} %add_add_fusion.own_ref, ...), custom_call_target="tpu_custom_call" | custom-call | flops 171966464 | bytes 10000000 | tf_op jit(solution)/shard_map/project_back/pallas_call | solution.py:374
  26.9 0.6 %collective-permute-start.9 = (f32[32,1536]{1,0:T(8,128)S(1)}, f32[32,1536]{1,0:T(8,128)S(1)}, u32[]{:S(2)}, u32[]{:S(2)}) collective-permute-start(f32[32,1536]{1,0:T(8,128)S(1)} %get-tuple-element.75), channel_id=1, source_target_pairs={{0,8},{4,12},{8,0},{12,4},{16,24},{20,28},{24,16},{28,20},{1,9},{5... | collective-permute-start | bytes 589832 | tf_op jit(solution)/shard_map/ppermute | solution.py:528
  27.5 1.5 %collective-permute-start.10 = (f32[32,1536]{1,0:T(8,128)S(1)}, f32[32,1536]{1,0:T(8,128)S(1)}, u32[]{:S(2)}, u32[]{:S(2)}) collective-permute-start(f32[32,1536]{1,0:T(8,128)S(1)} %get-tuple-element.77), channel_id=1, source_target_pairs={{0,16},{4,20},{8,24},{12,28},{16,0},{20,4},{24,8},{28,12},{1,17},{... | collective-permute-start | bytes 589832 | tf_op jit(solution)/shard_map/ppermute | solution.py:528
  29.0 1.5 %collective-permute-start.13 = (f32[32,1280]{1,0:T(8,128)S(1)}, f32[32,1280]{1,0:T(8,128)S(1)}, u32[]{:S(2)}, u32[]{:S(2)}) collective-permute-start(f32[32,1280]{1,0:T(8,128)S(1)} %get-tuple-element.83), channel_id=1, source_target_pairs={{0,8},{4,12},{8,0},{12,4},{16,24},{20,28},{24,16},{28,20},{1,9},{5... | collective-permute-start | bytes 491528 | tf_op jit(solution)/shard_map/ppermute | solution.py:528
  31.0 3.7 %collective-permute-done.9.refs_1_ = f32[32,1536]{1,0:T(8,128)S(1)} collective-permute-done((f32[32,1536]{1,0:T(8,128)S(1)}, f32[32,1536]{1,0:T(8,128)S(1)}, u32[]{:S(2)}, u32[]{:S(2)}) %collective-permute-start.9) | collective-permute-done | bytes 196640 | tf_op jit(solution)/shard_map/ppermute | solution.py:528
  34.7 0.6 %collective-permute-done.10.refs_3_ = f32[32,1536]{1,0:T(8,128)S(1)} collective-permute-done((f32[32,1536]{1,0:T(8,128)S(1)}, f32[32,1536]{1,0:T(8,128)S(1)}, u32[]{:S(2)}, u32[]{:S(2)}) %collective-permute-start.10) | collective-permute-done | bytes 196640 | tf_op jit(solution)/shard_map/ppermute | solution.py:528
  35.3 1.6 %collective-permute-start.11 = (f32[32,1536]{1,0:T(8,128)S(1)}, f32[32,1536]{1,0:T(8,128)S(1)}, u32[]{:S(2)}, u32[]{:S(2)}) collective-permute-start(f32[32,1536]{1,0:T(8,128)S(1)} %get-tuple-element.78.refs_0_), channel_id=1, source_target_pairs={{0,16},{4,20},{8,24},{12,28},{16,0},{20,4},{24,8},{28,12},{1,17},{... | collective-permute-start | bytes 589832 | tf_op jit(solution)/shard_map/ppermute | solution.py:528
  36.9 1.5 %collective-permute-start.12 = (f32[32,1536]{1,0:T(8,128)S(1)}, f32[32,1536]{1,0:T(8,128)S(1)}, u32[]{:S(2)}, u32[]{:S(2)}) collective-permute-start(f32[32,1536]{1,0:T(8,128)S(1)} %get-tuple-element.79.refs_2_), channel_id=1, source_target_pairs={{0,8},{4,12},{8,0},{12,4},{16,24},{20,28},{24,16},{28,20},{1,9},{5... | collective-permute-start | bytes 589832 | tf_op jit(solution)/shard_map/ppermute | solution.py:528
  38.5 1.4 %collective-permute-start.15 = (f32[32,1280]{1,0:T(8,128)S(1)}, f32[32,1280]{1,0:T(8,128)S(1)}, u32[]{:S(2)}, u32[]{:S(2)}) collective-permute-start(f32[32,1280]{1,0:T(8,128)S(1)} %get-tuple-element.86.refs_0_), channel_id=1, source_target_pairs={{0,16},{4,20},{8,24},{12,28},{16,0},{20,4},{24,8},{28,12},{1,17},{... | collective-permute-start | bytes 491528 | tf_op jit(solution)/shard_map/ppermute | solution.py:528
  39.9 0.6 %collective-permute-start.16 = (f32[32,896]{1,0:T(8,128)S(1)}, f32[32,896]{1,0:T(8,128)S(1)}, u32[]{:S(2)}, u32[]{:S(2)}) collective-permute-start(f32[32,896]{1,0:T(8,128)S(1)} %get-tuple-element.87.refs_2_), channel_id=1, source_target_pairs={{0,8},{4,12},{8,0},{12,4},{16,24},{20,28},{24,16},{28,20},{1,9},{5... | collective-permute-start | bytes 344072 | tf_op jit(solution)/shard_map/ppermute | solution.py:528
  40.5 2.3 %factor.1 = (f32[7,32,64]{2,1,0:T(8,128)}, bf16[7,32,96]{2,1,0:T(8,128)(2,1)S(1)}, bf16[7,64,96]{2,1,0:T(8,128)(2,1)S(1)}) custom-call(f32[7,32,64]{2,1,0:T(8,128)S(1)} %get-tuple-element.71.product_ref), custom_call_target="tpu_custom_call" | custom-call | flops 100000 | bytes 100000 | tf_op jit(solution)/shard_map/factor/pallas_call | solution.py:399
  42.8 1.2 %collective-permute-done.12.refs_3_ = f32[32,1536]{1,0:T(8,128)S(1)} collective-permute-done((f32[32,1536]{1,0:T(8,128)S(1)}, f32[32,1536]{1,0:T(8,128)S(1)}, u32[]{:S(2)}, u32[]{:S(2)}) %collective-permute-start.12) | collective-permute-done | bytes 196640 | tf_op jit(solution)/shard_map/ppermute | solution.py:528
  44.2 0.6 %collective-permute-start.17 = (f32[32,1536]{1,0:T(8,128)S(1)}, f32[32,1536]{1,0:T(8,128)S(1)}, u32[]{:S(2)}, u32[]{:S(2)}) collective-permute-start(f32[32,1536]{1,0:T(8,128)S(1)} %get-tuple-element.80.refs_0_), channel_id=1, source_target_pairs={{0,8},{4,12},{8,0},{12,4},{16,24},{20,28},{24,16},{28,20},{1,9},{5... | collective-permute-start | bytes 589832 | tf_op jit(solution)/shard_map/ppermute | solution.py:528
  44.9 1.0 %collective-permute-start.18 = (f32[32,1536]{1,0:T(8,128)S(1)}, f32[32,1536]{1,0:T(8,128)S(1)}, u32[]{:S(2)}, u32[]{:S(2)}) collective-permute-start(f32[32,1536]{1,0:T(8,128)S(1)} %get-tuple-element.81.refs_1_), channel_id=1, source_target_pairs={{0,16},{4,20},{8,24},{12,28},{16,0},{20,4},{24,8},{28,12},{1,17},{... | collective-permute-start | bytes 589832 | tf_op jit(solution)/shard_map/ppermute | solution.py:528
  46.7 0.6 %collective-permute-start.19 = (f32[32,1280]{1,0:T(8,128)S(1)}, f32[32,1280]{1,0:T(8,128)S(1)}, u32[]{:S(2)}, u32[]{:S(2)}) collective-permute-start(f32[32,1280]{1,0:T(8,128)S(1)} %get-tuple-element.90.refs_2_), channel_id=1, source_target_pairs={{0,8},{4,12},{8,0},{12,4},{16,24},{20,28},{24,16},{28,20},{1,9},{5... | collective-permute-start | bytes 491528 | tf_op jit(solution)/shard_map/ppermute | solution.py:528
  47.3 1.9 %collective-permute-start.20 = (f32[32,896]{1,0:T(8,128)S(1)}, f32[32,896]{1,0:T(8,128)S(1)}, u32[]{:S(2)}, u32[]{:S(2)}) collective-permute-start(f32[32,896]{1,0:T(8,128)S(1)} %get-tuple-element.91.refs_3_), channel_id=1, source_target_pairs={{0,16},{4,20},{8,24},{12,28},{16,0},{20,4},{24,8},{28,12},{1,17},{... | collective-permute-start | bytes 344072 | tf_op jit(solution)/shard_map/ppermute | solution.py:528
  49.3 1.6 %update_first.1 = (f32[1,3,64,2048]{3,2,1,0:T(8,128)}, f32[1,2,64,256]{3,2,1,0:T(8,128)}, f32[1,2,64,7168]{3,2,1,0:T(8,128)}, f32[3,32,2048]{2,1,0:T(8,128)}, f3...) custom-call(bf16[7,64,96]{2,1,0:T(8,128)(2,1)S(1)} %get-tuple-element.72.refs_0_, ...), custom_call_target="tpu_custom_call" | custom-call | flops 100000 | bytes 100000 | tf_op jit(solution)/shard_map/update_first/pallas_call | solution.py:507
  50.9 1.2 %collective-permute-done.20.refs_3_ = f32[32,896]{1,0:T(8,128)S(1)} collective-permute-done((f32[32,896]{1,0:T(8,128)S(1)}, f32[32,896]{1,0:T(8,128)S(1)}, u32[]{:S(2)}, u32[]{:S(2)}) %collective-permute-start.20) | collective-permute-done | bytes 114720 | tf_op jit(solution)/shard_map/ppermute | solution.py:528
  52.1 0.7 %collective-permute-done.19.refs_2_ = f32[32,1280]{1,0:T(8,128)S(1)} collective-permute-done((f32[32,1280]{1,0:T(8,128)S(1)}, f32[32,1280]{1,0:T(8,128)S(1)}, u32[]{:S(2)}, u32[]{:S(2)}) %collective-permute-start.19) | collective-permute-done | bytes 163872 | tf_op jit(solution)/shard_map/ppermute | solution.py:528
  52.9 2.3 %update_own.1 = (f32[1,3,64,2048]{3,2,1,0:T(8,128)}, f32[1,2,64,256]{3,2,1,0:T(8,128)}, f32[1,2,64,7168]{3,2,1,0:T(8,128)}, f32[3,32,2048]{2,1,0:T(8,128)}, f32[...) custom-call(bf16[7,64,96]{2,1,0:T(8,128)(2,1)S(1)} %get-tuple-elemen, ...), custom_call_target="tpu_custom_call", output_to_operand_aliasing={{0}: (4, {}), {1}: (5, {}), {2}: (6, {}), {3}: (7, {}), {4}... | custom-call | flops 100000 | bytes 40000000 | tf_op jit(solution)/shard_map/update_own/pallas_call | solution.py:507
  55.3 1.6 %update_other.1 = (f32[1,3,64,2048]{3,2,1,0:T(8,128)}, f32[1,2,64,256]{3,2,1,0:T(8,128)}, f32[1,2,64,7168]{3,2,1,0:T(8,128)}, f32[3,32,2048]{2,1,0:T(8,128)}, f3...) custom-call(bf16[7,64,96]{2,1,0:T(8,128)(2,1)S(1)} %get-tuple-elemen, ...), custom_call_target="tpu_custom_call", output_to_operand_aliasing={{0}: (3, {}), {1}: (4, {}), {2}: (5, {}), {3}: (6, {}), {4}... | custom-call | flops 100000 | bytes 40000000 | tf_op jit(solution)/shard_map/update_other/pallas_call | solution.py:507
  (31 shorter events, 4.1 us)
Async XLA Ops:
  6.1 1.4 %collective-permute-start = (f32[7,8,128]{2,1,0:T(8,128)S(1)}, f32[7,8,128]{2,1,0:T(8,128)S(1)}, u32[]{:S(2)}, u32[]{:S(2)}) collective-permute-start(f32[7,8,128]{2,1,0:T(8,128)S(1)} %get-tuple-element.66), channel_id=1, source_target_pairs={{0,4},{4,0},{8,12},{12,8},{16,20},{20,16},{24,28},{28,24},{1,5},{5... | collective-permute-start | bytes 86024 | tf_op jit(solution)/shard_map/ppermute | solution.py:528
  7.7 16.9 %collective-permute-start.1 = (f32[64,10496]{1,0:T(8,128)S(1)}, f32[64,10496]{1,0:T(8,128)S(1)}, u32[]{:S(2)}, u32[]{:S(2)}) collective-permute-start(f32[64,10496]{1,0:T(8,128)S(1)} %take_half.1), channel_id=1, source_target_pairs={{0,4},{4,0},{8,12},{12,8},{16,20},{20,16},{24,28},{28,24},{1,5},{5... | collective-permute-start | bytes 8060936 | tf_op jit(solution)/shard_map/ppermute | solution.py:528
  8.1 5.5 %collective-permute-start.4 = (f32[7,8,128]{2,1,0:T(8,128)S(1)}, f32[7,8,128]{2,1,0:T(8,128)S(1)}, u32[]{:S(2)}, u32[]{:S(2)}) collective-permute-start(f32[7,8,128]{2,1,0:T(8,128)S(1)} %add.21), channel_id=1, source_target_pairs={{0,24},{4,28},{8,16},{12,20},{16,8},{20,12},{24,0},{28,4},{1,25},{... | collective-permute-start | bytes 86024 | tf_op jit(solution)/shard_map/ppermute | solution.py:537
  11.7 3.9 %collective-permute-start.3 = (f32[7,8,128]{2,1,0:T(8,128)S(1)}, f32[7,8,128]{2,1,0:T(8,128)S(1)}, u32[]{:S(2)}, u32[]{:S(2)}) collective-permute-start(f32[7,8,128]{2,1,0:T(8,128)S(1)} %add.21), channel_id=1, source_target_pairs={{0,16},{4,20},{8,24},{12,28},{16,0},{20,4},{24,8},{28,12},{1,17},{... | collective-permute-start | bytes 86024 | tf_op jit(solution)/shard_map/ppermute | solution.py:537
  12.2 3.9 %collective-permute-start.2 = (f32[7,8,128]{2,1,0:T(8,128)S(1)}, f32[7,8,128]{2,1,0:T(8,128)S(1)}, u32[]{:S(2)}, u32[]{:S(2)}) collective-permute-start(f32[7,8,128]{2,1,0:T(8,128)S(1)} %add.21), channel_id=1, source_target_pairs={{0,8},{4,12},{8,0},{12,4},{16,24},{20,28},{24,16},{28,20},{1,9},{5... | collective-permute-start | bytes 86024 | tf_op jit(solution)/shard_map/ppermute | solution.py:537
  16.1 5.8 %collective-permute-start.7 = (f32[7,8,128]{2,1,0:T(8,128)S(1)}, f32[7,8,128]{2,1,0:T(8,128)S(1)}, u32[]{:S(2)}, u32[]{:S(2)}) collective-permute-start(f32[7,8,128]{2,1,0:T(8,128)S(1)} %add_add_fusion.1), channel_id=1, source_target_pairs={{0,3},{1,2},{2,1},{3,0},{4,7},{5,6},{6,5},{7,4},{8,11},{9,10},{10,... | collective-permute-start | bytes 86024 | tf_op jit(solution)/shard_map/ppermute | solution.py:537
  19.7 4.8 %collective-permute-start.6 = (f32[7,8,128]{2,1,0:T(8,128)S(1)}, f32[7,8,128]{2,1,0:T(8,128)S(1)}, u32[]{:S(2)}, u32[]{:S(2)}) collective-permute-start(f32[7,8,128]{2,1,0:T(8,128)S(1)} %add_add_fusion.1), channel_id=1, source_target_pairs={{0,2},{1,3},{2,0},{3,1},{4,6},{5,7},{6,4},{7,5},{8,10},{9,11},{10,... | collective-permute-start | bytes 86024 | tf_op jit(solution)/shard_map/ppermute | solution.py:537
  19.7 4.8 %collective-permute-start.5 = (f32[7,8,128]{2,1,0:T(8,128)S(1)}, f32[7,8,128]{2,1,0:T(8,128)S(1)}, u32[]{:S(2)}, u32[]{:S(2)}) collective-permute-start(f32[7,8,128]{2,1,0:T(8,128)S(1)} %add_add_fusion.1), channel_id=1, source_target_pairs={{0,1},{1,0},{2,3},{3,2},{4,5},{5,4},{6,7},{7,6},{8,9},{9,8},{10,11... | collective-permute-start | bytes 86024 | tf_op jit(solution)/shard_map/ppermute | solution.py:537
  24.5 1.3 %collective-permute-start.8 = (f32[7,8,128]{2,1,0:T(8,128)S(1)}, f32[7,8,128]{2,1,0:T(8,128)S(1)}, u32[]{:S(2)}, u32[]{:S(2)}) collective-permute-start(f32[7,8,128]{2,1,0:T(8,128)S(1)} %add_add_fusion.own_ref), channel_id=1, source_target_pairs={{0,4},{4,0},{8,12},{12,8},{16,20},{20,16},{24,28},{28,24},{1,5},{5... | collective-permute-start | bytes 86024 | tf_op jit(solution)/shard_map/ppermute | solution.py:528
  26.9 7.8 %collective-permute-start.9 = (f32[32,1536]{1,0:T(8,128)S(1)}, f32[32,1536]{1,0:T(8,128)S(1)}, u32[]{:S(2)}, u32[]{:S(2)}) collective-permute-start(f32[32,1536]{1,0:T(8,128)S(1)} %get-tuple-element.75), channel_id=1, source_target_pairs={{0,8},{4,12},{8,0},{12,4},{16,24},{20,28},{24,16},{28,20},{1,9},{5... | collective-permute-start | bytes 589832 | tf_op jit(solution)/shard_map/ppermute | solution.py:528
  27.5 7.8 %collective-permute-start.10 = (f32[32,1536]{1,0:T(8,128)S(1)}, f32[32,1536]{1,0:T(8,128)S(1)}, u32[]{:S(2)}, u32[]{:S(2)}) collective-permute-start(f32[32,1536]{1,0:T(8,128)S(1)} %get-tuple-element.77), channel_id=1, source_target_pairs={{0,16},{4,20},{8,24},{12,28},{16,0},{20,4},{24,8},{28,12},{1,17},{... | collective-permute-start | bytes 589832 | tf_op jit(solution)/shard_map/ppermute | solution.py:528
  29.0 9.4 %collective-permute-start.13 = (f32[32,1280]{1,0:T(8,128)S(1)}, f32[32,1280]{1,0:T(8,128)S(1)}, u32[]{:S(2)}, u32[]{:S(2)}) collective-permute-start(f32[32,1280]{1,0:T(8,128)S(1)} %get-tuple-element.83), channel_id=1, source_target_pairs={{0,8},{4,12},{8,0},{12,4},{16,24},{20,28},{24,16},{28,20},{1,9},{5... | collective-permute-start | bytes 491528 | tf_op jit(solution)/shard_map/ppermute | solution.py:528
  30.5 7.9 %collective-permute-start.14 = (f32[32,896]{1,0:T(8,128)S(1)}, f32[32,896]{1,0:T(8,128)S(1)}, u32[]{:S(2)}, u32[]{:S(2)}) collective-permute-start(f32[32,896]{1,0:T(8,128)S(1)} %get-tuple-element.85), channel_id=1, source_target_pairs={{0,16},{4,20},{8,24},{12,28},{16,0},{20,4},{24,8},{28,12},{1,17},{... | collective-permute-start | bytes 344072 | tf_op jit(solution)/shard_map/ppermute | solution.py:528
  35.3 7.4 %collective-permute-start.11 = (f32[32,1536]{1,0:T(8,128)S(1)}, f32[32,1536]{1,0:T(8,128)S(1)}, u32[]{:S(2)}, u32[]{:S(2)}) collective-permute-start(f32[32,1536]{1,0:T(8,128)S(1)} %get-tuple-element.78.refs_0_), channel_id=1, source_target_pairs={{0,16},{4,20},{8,24},{12,28},{16,0},{20,4},{24,8},{28,12},{1,17},{... | collective-permute-start | bytes 589832 | tf_op jit(solution)/shard_map/ppermute | solution.py:528
  36.9 7.1 %collective-permute-start.12 = (f32[32,1536]{1,0:T(8,128)S(1)}, f32[32,1536]{1,0:T(8,128)S(1)}, u32[]{:S(2)}, u32[]{:S(2)}) collective-permute-start(f32[32,1536]{1,0:T(8,128)S(1)} %get-tuple-element.79.refs_2_), channel_id=1, source_target_pairs={{0,8},{4,12},{8,0},{12,4},{16,24},{20,28},{24,16},{28,20},{1,9},{5... | collective-permute-start | bytes 589832 | tf_op jit(solution)/shard_map/ppermute | solution.py:528
  38.5 8.0 %collective-permute-start.15 = (f32[32,1280]{1,0:T(8,128)S(1)}, f32[32,1280]{1,0:T(8,128)S(1)}, u32[]{:S(2)}, u32[]{:S(2)}) collective-permute-start(f32[32,1280]{1,0:T(8,128)S(1)} %get-tuple-element.86.refs_0_), channel_id=1, source_target_pairs={{0,16},{4,20},{8,24},{12,28},{16,0},{20,4},{24,8},{28,12},{1,17},{... | collective-permute-start | bytes 491528 | tf_op jit(solution)/shard_map/ppermute | solution.py:528
  39.9 6.6 %collective-permute-start.16 = (f32[32,896]{1,0:T(8,128)S(1)}, f32[32,896]{1,0:T(8,128)S(1)}, u32[]{:S(2)}, u32[]{:S(2)}) collective-permute-start(f32[32,896]{1,0:T(8,128)S(1)} %get-tuple-element.87.refs_2_), channel_id=1, source_target_pairs={{0,8},{4,12},{8,0},{12,4},{16,24},{20,28},{24,16},{28,20},{1,9},{5... | collective-permute-start | bytes 344072 | tf_op jit(solution)/shard_map/ppermute | solution.py:528
  44.2 8.6 %collective-permute-start.17 = (f32[32,1536]{1,0:T(8,128)S(1)}, f32[32,1536]{1,0:T(8,128)S(1)}, u32[]{:S(2)}, u32[]{:S(2)}) collective-permute-start(f32[32,1536]{1,0:T(8,128)S(1)} %get-tuple-element.80.refs_0_), channel_id=1, source_target_pairs={{0,8},{4,12},{8,0},{12,4},{16,24},{20,28},{24,16},{28,20},{1,9},{5... | collective-permute-start | bytes 589832 | tf_op jit(solution)/shard_map/ppermute | solution.py:528
  44.9 7.9 %collective-permute-start.18 = (f32[32,1536]{1,0:T(8,128)S(1)}, f32[32,1536]{1,0:T(8,128)S(1)}, u32[]{:S(2)}, u32[]{:S(2)}) collective-permute-start(f32[32,1536]{1,0:T(8,128)S(1)} %get-tuple-element.81.refs_1_), channel_id=1, source_target_pairs={{0,16},{4,20},{8,24},{12,28},{16,0},{20,4},{24,8},{28,12},{1,17},{... | collective-permute-start | bytes 589832 | tf_op jit(solution)/shard_map/ppermute | solution.py:528
  46.7 6.1 %collective-permute-start.19 = (f32[32,1280]{1,0:T(8,128)S(1)}, f32[32,1280]{1,0:T(8,128)S(1)}, u32[]{:S(2)}, u32[]{:S(2)}) collective-permute-start(f32[32,1280]{1,0:T(8,128)S(1)} %get-tuple-element.90.refs_2_), channel_id=1, source_target_pairs={{0,8},{4,12},{8,0},{12,4},{16,24},{20,28},{24,16},{28,20},{1,9},{5... | collective-permute-start | bytes 491528 | tf_op jit(solution)/shard_map/ppermute | solution.py:528
  47.3 4.8 %collective-permute-start.20 = (f32[32,896]{1,0:T(8,128)S(1)}, f32[32,896]{1,0:T(8,128)S(1)}, u32[]{:S(2)}, u32[]{:S(2)}) collective-permute-start(f32[32,896]{1,0:T(8,128)S(1)} %get-tuple-element.91.refs_3_), channel_id=1, source_target_pairs={{0,16},{4,20},{8,24},{12,28},{16,0},{20,4},{24,8},{28,12},{1,17},{... | collective-permute-start | bytes 344072 | tf_op jit(solution)/shard_map/ppermute | solution.py:528
  49.2 3.7 %collective-permute-start.22 = (f32[32,5248]{1,0:T(8,128)S(1)}, f32[32,5248]{1,0:T(8,128)S(1)}, u32[]{:S(2)}, u32[]{:S(2)}) collective-permute-start(f32[32,5248]{1,0:T(8,128)S(1)} %pack.2.refs_2_), channel_id=1, source_target_pairs={{0,4},{4,0},{8,12},{12,8},{16,20},{20,16},{24,28},{28,24},{1,5},{5... | collective-permute-start | bytes 2015240 | tf_op jit(solution)/shard_map/ppermute | solution.py:528
  52.8 2.4 %collective-permute-start.21 = (f32[32,5248]{1,0:T(8,128)S(1)}, f32[32,5248]{1,0:T(8,128)S(1)}, u32[]{:S(2)}, u32[]{:S(2)}) collective-permute-start(f32[32,5248]{1,0:T(8,128)S(1)} %pack.3.refs_2_), channel_id=1, source_target_pairs={{0,4},{4,0},{8,12},{12,8},{16,20},{20,16},{24,28},{28,24},{1,5},{5... | collective-permute-start | bytes 2015240 | tf_op jit(solution)/shard_map/ppermute | solution.py:528
